TPU v7x, 32 devices: a whole 2x2x4 slice. The times are simulated.
32 devices in a mesh: depth: 4 (over x, core), lat: 8 (over z, y).
Axes of the slice: x: 2, y: 2, z: 4, core: 2. Of those that a mesh axis runs over, the one named last changes fastest.
Arguments:
- source_field: float32 [2, 4, 256, 1024], P(None, None, 'lat'), may hold values from -9 to 9, as said below
- receiver_field: float32 [2, 4, 256, 1024], P(None, None, 'lat'), may hold values from -9 to 9, as said below
- zone_index: int32 [16, 256, 1024], P('depth', 'lat'), may hold values from 0 to 2
- blend_weight: int32 [16, 256, 1024], P('depth', 'lat'), may hold values from 0 to 16
- ref_velocity: float32 [4], replicated, may hold values from 1500 to 4500
- frequencies: int32 [4], replicated, may hold values from 5 to 40
Outputs:
- migrated_image: float32 [16, 256, 1024], P('depth', 'lat')
Inputs may be any that keep to these rules, and one draw needn't show every extreme that they name: `source_field`: surface wavefields of order one. `receiver_field`: recorded wavefields of order one.
All inputs are finite; a program needn't handle non-finite values.
Results may differ from a plain program's by a relative error of at most 0.0003.
Values sent between devices are 32-bit elements; how exact they have to be, the bound alone decides.
No kernel may reach another device: no remote copies, remote signals or barrier semaphores. Data moves between devices by JAX's collectives and lax.ppermute only.
A program may use at most 64 MiB of HBM per device.

v0:
```python
import math

import jax
import jax.numpy as jnp
from jax import lax
from jax.sharding import PartitionSpec as P

HALF = 7
BLEND = 16


cell_width = 5.0
depth_step = 10.0
taper_width = 16.0


def padded_2(block, sides, width):
    for axis, dim in sides:
        count = lax.axis_size(axis)
        forward = [(i, i + 1) for i in range(count - 1)]
        backward = [(target, source) for source, target in forward]
        low = lax.ppermute(
            lax.slice_in_dim(block, block.shape[dim] - width, None, axis=dim), axis, forward
        )
        high = lax.ppermute(lax.slice_in_dim(block, 0, width, axis=dim), axis, backward)
        block = jnp.concatenate([low, block, high], axis=dim)
    return block


def kernels(frequencies, ref_velocity):
    offsets = jnp.arange(-HALF, HALF + 1, dtype=jnp.int32).astype(jnp.float32)
    wavenumber = 2.0 * math.pi * frequencies.astype(jnp.float32)[:, None] / ref_velocity[None, :]
    curvature = wavenumber * (cell_width * cell_width / (2.0 * depth_step))
    phase_turn = wavenumber * depth_step
    chirp_angle = curvature[:, :, None] * (offsets * offsets)[None, None, :]
    envelope = jnp.exp(-offsets * offsets / taper_width)
    raw_re = envelope * jnp.cos(chirp_angle)
    raw_im = envelope * jnp.sin(chirp_angle)
    magnitude = jnp.sqrt(jnp.sum(raw_re, axis=-1) ** 2 + jnp.sum(raw_im, axis=-1) ** 2)[:, :, None]
    return (raw_re / magnitude, raw_im / magnitude, jnp.cos(phase_turn), jnp.sin(phase_turn))


def convolve_rows(real, imag, tap_re, tap_im):
    length = real.shape[0] - 2 * HALF
    out_re = jnp.zeros((tap_re.shape[0], length, real.shape[1]), jnp.float32)
    out_im = jnp.zeros((tap_re.shape[0], length, real.shape[1]), jnp.float32)
    for offset in range(2 * HALF + 1):
        part_re = real[offset : offset + length][None]
        part_im = imag[offset : offset + length][None]
        coef_re = tap_re[:, offset][:, None, None]
        coef_im = tap_im[:, offset][:, None, None]
        out_re = out_re + coef_re * part_re - coef_im * part_im
        out_im = out_im + coef_re * part_im + coef_im * part_re
    return (out_re, out_im)


def convolve_cols(real, imag, tap_re, tap_im):
    length = real.shape[2] - 2 * HALF
    out_re = jnp.zeros(real.shape[:2] + (length,), jnp.float32)
    out_im = jnp.zeros(real.shape[:2] + (length,), jnp.float32)
    for offset in range(2 * HALF + 1):
        part_re = real[:, :, offset : offset + length]
        part_im = imag[:, :, offset : offset + length]
        coef_re = tap_re[:, offset][:, None, None]
        coef_im = tap_im[:, offset][:, None, None]
        out_re = out_re + coef_re * part_re - coef_im * part_im
        out_im = out_im + coef_re * part_im + coef_im * part_re
    return (out_re, out_im)


def advance(pad_re, pad_im, tap_re, tap_im, turn_cos, turn_sin, zone_level, weight_level):
    rows_re, rows_im = convolve_rows(pad_re, pad_im, tap_re, tap_im)
    widths = ((0, 0), (0, 0), (HALF, HALF))
    both_re, both_im = convolve_cols(
        jnp.pad(rows_re, widths), jnp.pad(rows_im, widths), tap_re, tap_im
    )
    phased_re = both_re * turn_cos[:, None, None] - both_im * turn_sin[:, None, None]
    phased_im = both_re * turn_sin[:, None, None] + both_im * turn_cos[:, None, None]
    reference_ids = jnp.arange(tap_re.shape[0], dtype=jnp.int32)[:, None, None]
    weights = jnp.where(reference_ids == zone_level[None], 1.0 - weight_level[None], 0.0)
    weights = weights + jnp.where(reference_ids == zone_level[None] + 1, weight_level[None], 0.0)
    return (jnp.sum(weights * phased_re, axis=0), jnp.sum(weights * phased_im, axis=0))


def local(source_field, receiver_field, zone_index, blend_weight, ref_velocity, frequencies):
    tap_re, tap_im, turn_cos, turn_sin = kernels(frequencies, ref_velocity)
    group_index = lax.axis_index("depth")
    groups = lax.axis_size("depth")
    freq_count = source_field.shape[1]
    surface = jnp.stack([source_field[0], source_field[1], receiver_field[0], receiver_field[1]])

    def single_step(padded, which, zone_level, weight_level):
        source_re, source_im = advance(
            padded[0],
            padded[1],
            tap_re[which],
            tap_im[which],
            turn_cos[which],
            turn_sin[which],
            zone_level,
            weight_level,
        )
        receiver_re, receiver_im = advance(
            padded[2],
            padded[3],
            tap_re[which],
            -tap_im[which],
            turn_cos[which],
            -turn_sin[which],
            zone_level,
            weight_level,
        )
        return jnp.stack([source_re, source_im, receiver_re, receiver_im])

    per_group = freq_count // groups
    first = group_index * per_group
    chosen_block = first + jnp.arange(per_group, dtype=jnp.int32)
    block_fields = lax.dynamic_slice_in_dim(surface, first, per_group, 1)
    zone_whole, blend_whole = (
        lax.all_gather(zone_index, "depth", axis=0, tiled=True),
        lax.all_gather(blend_weight, "depth", axis=0, tiled=True),
    )

    def each_level(current, tables):
        zone_level, weight_level = tables
        padded = padded_2(current, (("lat", 2),), HALF)
        stepped = jax.vmap(single_step, in_axes=(1, 0, None, None), out_axes=1)(
            padded, chosen_block, zone_level, weight_level
        )
        return (stepped, stepped[0] * stepped[2] + stepped[1] * stepped[3])

    _, pieces = lax.scan(
        each_level, block_fields, (zone_whole, blend_whole.astype(jnp.float32) / BLEND)
    )
    migrated = lax.psum_scatter(jnp.sum(pieces, axis=1), "depth", scatter_dimension=0, tiled=True)
    return migrated / freq_count


def solution(mesh):
    in_specs = (
        P(None, None, "lat", None),
        P(None, None, "lat", None),
        P("depth", "lat", None),
        P("depth", "lat", None),
        P(),
        P(),
    )
    out_specs = P("depth", "lat", None)
    return jax.shard_map(local, mesh=mesh, in_specs=in_specs, out_specs=out_specs, check_vma=False)
```

profile of v0, /device:TPU:0, one launch (start us, length us, event | category | flops | bytes accessed | tf_op | source)
XLA Modules:
  0.0 681.7 jit_solution(12780838671425919798)
XLA Ops:
  12.8 21.4 %all-gather.5.cloned.1.call-done = s32[16,32,1024]{2,1,0:T(8,128)} async-done(((s32[4,32,1024]{2,1,0:T(8,128)}), s32[16,32,1024]{2,1,0:T(8,128)}) %all-gather.5.cloned.1.call-update) | async-done | bytes 2097168 | tf_op jit(solution)/shard_map/all_gather | solution.py:121
  36.1 22.4 %all-gather.3.cloned.1.call-done = s32[16,32,1024]{2,1,0:T(8,128)} async-done(((s32[4,32,1024]{2,1,0:T(8,128)}), s32[16,32,1024]{2,1,0:T(8,128)}) %all-gather.3.cloned.1.call-update) | async-done | bytes 2097168 | tf_op jit(solution)/shard_map/all_gather | solution.py:120
  58.4 583.2 %while.21 = (s32[]{:T(128)}, f32[4,1,32,1024]{3,2,1,0:T(8,128)S(1)}, f32[16,1,32,1024]{3,2,1,0:T(8,128)}, s32[16,32,1024]{2,1,0:T(8,128)}, f32[16,32,1024]{2,1,0...) while((s32[]{:T(128)}, ...), condition=%wide.region_7.8_spmd, body=%wide.region_2.7_spmd.sunk | while | flops 65945600 | bytes 43588636 | solution.py:132
  77.4 15.9 %multiply_reduce_fusion.5 = (f32[32,1024]{1,0:T(8,128)S(1)}, f32[32,1024]{1,0:T(8,128)S(1)}, f32[32,1024]{1,0:T(8,128)S(1)}, f32[32,1024]{1,0:T(8,128)S(1)}) fusion(f32[4]{0:T(128)S(1)} %bitcast.246, f32[4]{0:T(128)S(1)} %bitcast.247, f32[32,1024]{1,0:T(8,128)S(1)} %get-tuple-element.689, s32[32,1024]{1,0:T(8,128)S(1)} %get-tuple-element.690, ...), kind=kLoop, calls=%fused_computation.65.clone.1 | loop fusion | flops 34078720 | bytes 3146496 | tf_op jit(solution)/shard_map/while/body/eval_jaxpr/vmap()/reduce_sum | solution.py:82
  96.1 5.0 collective-permute-start.1
  113.9 15.9 %multiply_reduce_fusion.5 = (f32[32,1024]{1,0:T(8,128)S(1)}, f32[32,1024]{1,0:T(8,128)S(1)}, f32[32,1024]{1,0:T(8,128)S(1)}, f32[32,1024]{1,0:T(8,128)S(1)}) fusion(f32[4]{0:T(128)S(1)} %bitcast.246, f32[4]{0:T(128)S(1)} %bitcast.247, f32[32,1024]{1,0:T(8,128)S(1)} %get-tuple-element.689, s32[32,1024]{1,0:T(8,128)S(1)} %get-tuple-element.690, ...), kind=kLoop, calls=%fused_computation.65.clone.1 | loop fusion | flops 34078720 | bytes 3146496 | tf_op jit(solution)/shard_map/while/body/eval_jaxpr/vmap()/reduce_sum | solution.py:82
  132.6 5.0 collective-permute-start.1
  150.4 15.9 %multiply_reduce_fusion.5 = (f32[32,1024]{1,0:T(8,128)S(1)}, f32[32,1024]{1,0:T(8,128)S(1)}, f32[32,1024]{1,0:T(8,128)S(1)}, f32[32,1024]{1,0:T(8,128)S(1)}) fusion(f32[4]{0:T(128)S(1)} %bitcast.246, f32[4]{0:T(128)S(1)} %bitcast.247, f32[32,1024]{1,0:T(8,128)S(1)} %get-tuple-element.689, s32[32,1024]{1,0:T(8,128)S(1)} %get-tuple-element.690, ...), kind=kLoop, calls=%fused_computation.65.clone.1 | loop fusion | flops 34078720 | bytes 3146496 | tf_op jit(solution)/shard_map/while/body/eval_jaxpr/vmap()/reduce_sum | solution.py:82
  169.1 5.0 collective-permute-start.1
  186.9 15.9 %multiply_reduce_fusion.5 = (f32[32,1024]{1,0:T(8,128)S(1)}, f32[32,1024]{1,0:T(8,128)S(1)}, f32[32,1024]{1,0:T(8,128)S(1)}, f32[32,1024]{1,0:T(8,128)S(1)}) fusion(f32[4]{0:T(128)S(1)} %bitcast.246, f32[4]{0:T(128)S(1)} %bitcast.247, f32[32,1024]{1,0:T(8,128)S(1)} %get-tuple-element.689, s32[32,1024]{1,0:T(8,128)S(1)} %get-tuple-element.690, ...), kind=kLoop, calls=%fused_computation.65.clone.1 | loop fusion | flops 34078720 | bytes 3146496 | tf_op jit(solution)/shard_map/while/body/eval_jaxpr/vmap()/reduce_sum | solution.py:82
  205.6 5.0 collective-permute-start.1
  223.4 15.9 %multiply_reduce_fusion.5 = (f32[32,1024]{1,0:T(8,128)S(1)}, f32[32,1024]{1,0:T(8,128)S(1)}, f32[32,1024]{1,0:T(8,128)S(1)}, f32[32,1024]{1,0:T(8,128)S(1)}) fusion(f32[4]{0:T(128)S(1)} %bitcast.246, f32[4]{0:T(128)S(1)} %bitcast.247, f32[32,1024]{1,0:T(8,128)S(1)} %get-tuple-element.689, s32[32,1024]{1,0:T(8,128)S(1)} %get-tuple-element.690, ...), kind=kLoop, calls=%fused_computation.65.clone.1 | loop fusion | flops 34078720 | bytes 3146496 | tf_op jit(solution)/shard_map/while/body/eval_jaxpr/vmap()/reduce_sum | solution.py:82
  242.1 5.0 collective-permute-start.1
  259.9 15.9 %multiply_reduce_fusion.5 = (f32[32,1024]{1,0:T(8,128)S(1)}, f32[32,1024]{1,0:T(8,128)S(1)}, f32[32,1024]{1,0:T(8,128)S(1)}, f32[32,1024]{1,0:T(8,128)S(1)}) fusion(f32[4]{0:T(128)S(1)} %bitcast.246, f32[4]{0:T(128)S(1)} %bitcast.247, f32[32,1024]{1,0:T(8,128)S(1)} %get-tuple-element.689, s32[32,1024]{1,0:T(8,128)S(1)} %get-tuple-element.690, ...), kind=kLoop, calls=%fused_computation.65.clone.1 | loop fusion | flops 34078720 | bytes 3146496 | tf_op jit(solution)/shard_map/while/body/eval_jaxpr/vmap()/reduce_sum | solution.py:82
  278.6 5.0 collective-permute-start.1
  296.4 15.9 %multiply_reduce_fusion.5 = (f32[32,1024]{1,0:T(8,128)S(1)}, f32[32,1024]{1,0:T(8,128)S(1)}, f32[32,1024]{1,0:T(8,128)S(1)}, f32[32,1024]{1,0:T(8,128)S(1)}) fusion(f32[4]{0:T(128)S(1)} %bitcast.246, f32[4]{0:T(128)S(1)} %bitcast.247, f32[32,1024]{1,0:T(8,128)S(1)} %get-tuple-element.689, s32[32,1024]{1,0:T(8,128)S(1)} %get-tuple-element.690, ...), kind=kLoop, calls=%fused_computation.65.clone.1 | loop fusion | flops 34078720 | bytes 3146496 | tf_op jit(solution)/shard_map/while/body/eval_jaxpr/vmap()/reduce_sum | solution.py:82
  315.1 5.0 collective-permute-start.1
  332.9 15.9 %multiply_reduce_fusion.5 = (f32[32,1024]{1,0:T(8,128)S(1)}, f32[32,1024]{1,0:T(8,128)S(1)}, f32[32,1024]{1,0:T(8,128)S(1)}, f32[32,1024]{1,0:T(8,128)S(1)}) fusion(f32[4]{0:T(128)S(1)} %bitcast.246, f32[4]{0:T(128)S(1)} %bitcast.247, f32[32,1024]{1,0:T(8,128)S(1)} %get-tuple-element.689, s32[32,1024]{1,0:T(8,128)S(1)} %get-tuple-element.690, ...), kind=kLoop, calls=%fused_computation.65.clone.1 | loop fusion | flops 34078720 | bytes 3146496 | tf_op jit(solution)/shard_map/while/body/eval_jaxpr/vmap()/reduce_sum | solution.py:82
  351.6 5.0 collective-permute-start.1
  369.4 15.9 %multiply_reduce_fusion.5 = (f32[32,1024]{1,0:T(8,128)S(1)}, f32[32,1024]{1,0:T(8,128)S(1)}, f32[32,1024]{1,0:T(8,128)S(1)}, f32[32,1024]{1,0:T(8,128)S(1)}) fusion(f32[4]{0:T(128)S(1)} %bitcast.246, f32[4]{0:T(128)S(1)} %bitcast.247, f32[32,1024]{1,0:T(8,128)S(1)} %get-tuple-element.689, s32[32,1024]{1,0:T(8,128)S(1)} %get-tuple-element.690, ...), kind=kLoop, calls=%fused_computation.65.clone.1 | loop fusion | flops 34078720 | bytes 3146496 | tf_op jit(solution)/shard_map/while/body/eval_jaxpr/vmap()/reduce_sum | solution.py:82
  388.1 5.0 collective-permute-start.1
  405.9 15.9 %multiply_reduce_fusion.5 = (f32[32,1024]{1,0:T(8,128)S(1)}, f32[32,1024]{1,0:T(8,128)S(1)}, f32[32,1024]{1,0:T(8,128)S(1)}, f32[32,1024]{1,0:T(8,128)S(1)}) fusion(f32[4]{0:T(128)S(1)} %bitcast.246, f32[4]{0:T(128)S(1)} %bitcast.247, f32[32,1024]{1,0:T(8,128)S(1)} %get-tuple-element.689, s32[32,1024]{1,0:T(8,128)S(1)} %get-tuple-element.690, ...), kind=kLoop, calls=%fused_computation.65.clone.1 | loop fusion | flops 34078720 | bytes 3146496 | tf_op jit(solution)/shard_map/while/body/eval_jaxpr/vmap()/reduce_sum | solution.py:82
  424.6 5.0 collective-permute-start.1
  442.4 15.9 %multiply_reduce_fusion.5 = (f32[32,1024]{1,0:T(8,128)S(1)}, f32[32,1024]{1,0:T(8,128)S(1)}, f32[32,1024]{1,0:T(8,128)S(1)}, f32[32,1024]{1,0:T(8,128)S(1)}) fusion(f32[4]{0:T(128)S(1)} %bitcast.246, f32[4]{0:T(128)S(1)} %bitcast.247, f32[32,1024]{1,0:T(8,128)S(1)} %get-tuple-element.689, s32[32,1024]{1,0:T(8,128)S(1)} %get-tuple-element.690, ...), kind=kLoop, calls=%fused_computation.65.clone.1 | loop fusion | flops 34078720 | bytes 3146496 | tf_op jit(solution)/shard_map/while/body/eval_jaxpr/vmap()/reduce_sum | solution.py:82
  461.1 5.0 collective-permute-start.1
  478.9 15.9 %multiply_reduce_fusion.5 = (f32[32,1024]{1,0:T(8,128)S(1)}, f32[32,1024]{1,0:T(8,128)S(1)}, f32[32,1024]{1,0:T(8,128)S(1)}, f32[32,1024]{1,0:T(8,128)S(1)}) fusion(f32[4]{0:T(128)S(1)} %bitcast.246, f32[4]{0:T(128)S(1)} %bitcast.247, f32[32,1024]{1,0:T(8,128)S(1)} %get-tuple-element.689, s32[32,1024]{1,0:T(8,128)S(1)} %get-tuple-element.690, ...), kind=kLoop, calls=%fused_computation.65.clone.1 | loop fusion | flops 34078720 | bytes 3146496 | tf_op jit(solution)/shard_map/while/body/eval_jaxpr/vmap()/reduce_sum | solution.py:82
  515.4 15.9 %multiply_reduce_fusion.5 = (f32[32,1024]{1,0:T(8,128)S(1)}, f32[32,1024]{1,0:T(8,128)S(1)}, f32[32,1024]{1,0:T(8,128)S(1)}, f32[32,1024]{1,0:T(8,128)S(1)}) fusion(f32[4]{0:T(128)S(1)} %bitcast.246, f32[4]{0:T(128)S(1)} %bitcast.247, f32[32,1024]{1,0:T(8,128)S(1)} %get-tuple-element.689, s32[32,1024]{1,0:T(8,128)S(1)} %get-tuple-element.690, ...), kind=kLoop, calls=%fused_computation.65.clone.1 | loop fusion | flops 34078720 | bytes 3146496 | tf_op jit(solution)/shard_map/while/body/eval_jaxpr/vmap()/reduce_sum | solution.py:82
  551.9 15.9 %multiply_reduce_fusion.5 = (f32[32,1024]{1,0:T(8,128)S(1)}, f32[32,1024]{1,0:T(8,128)S(1)}, f32[32,1024]{1,0:T(8,128)S(1)}, f32[32,1024]{1,0:T(8,128)S(1)}) fusion(f32[4]{0:T(128)S(1)} %bitcast.246, f32[4]{0:T(128)S(1)} %bitcast.247, f32[32,1024]{1,0:T(8,128)S(1)} %get-tuple-element.689, s32[32,1024]{1,0:T(8,128)S(1)} %get-tuple-element.690, ...), kind=kLoop, calls=%fused_computation.65.clone.1 | loop fusion | flops 34078720 | bytes 3146496 | tf_op jit(solution)/shard_map/while/body/eval_jaxpr/vmap()/reduce_sum | solution.py:82
  570.6 5.0 collective-permute-start.1
  588.4 15.9 %multiply_reduce_fusion.5 = (f32[32,1024]{1,0:T(8,128)S(1)}, f32[32,1024]{1,0:T(8,128)S(1)}, f32[32,1024]{1,0:T(8,128)S(1)}, f32[32,1024]{1,0:T(8,128)S(1)}) fusion(f32[4]{0:T(128)S(1)} %bitcast.246, f32[4]{0:T(128)S(1)} %bitcast.247, f32[32,1024]{1,0:T(8,128)S(1)} %get-tuple-element.689, s32[32,1024]{1,0:T(8,128)S(1)} %get-tuple-element.690, ...), kind=kLoop, calls=%fused_computation.65.clone.1 | loop fusion | flops 34078720 | bytes 3146496 | tf_op jit(solution)/shard_map/while/body/eval_jaxpr/vmap()/reduce_sum | solution.py:82
  624.9 15.9 %multiply_reduce_fusion.5 = (f32[32,1024]{1,0:T(8,128)S(1)}, f32[32,1024]{1,0:T(8,128)S(1)}, f32[32,1024]{1,0:T(8,128)S(1)}, f32[32,1024]{1,0:T(8,128)S(1)}) fusion(f32[4]{0:T(128)S(1)} %bitcast.246, f32[4]{0:T(128)S(1)} %bitcast.247, f32[32,1024]{1,0:T(8,128)S(1)} %get-tuple-element.689, s32[32,1024]{1,0:T(8,128)S(1)} %get-tuple-element.690, ...), kind=kLoop, calls=%fused_computation.65.clone.1 | loop fusion | flops 34078720 | bytes 3146496 | tf_op jit(solution)/shard_map/while/body/eval_jaxpr/vmap()/reduce_sum | solution.py:82
  641.6 31.7 %reduce-scatter.2.cloned.1.call-done = f32[4,32,1024]{2,1,0:T(8,128)} async-done(((f32[16,32,1024]{2,1,0:T(8,128)}), f32[4,32,1024]{2,1,0:T(8,128)}) %reduce-scatter.2.cloned.1.call-update) | async-done | bytes 524304 | tf_op jit(solution)/shard_map/reduce_scatter | solution.py:135
  (1353 shorter events, 270.4 us)
Async XLA Ops:
  6.5 27.7 %all-gather.5.cloned.1.call-start = ((), (), s32[]{:S(2)}) async-start(), calls=%async_computation.2 | async-start | bytes 2621440 | tf_op jit(solution)/shard_map/all_gather | solution.py:121
  7.3 51.2 %all-gather.3.cloned.1.call-start = ((), (), s32[]{:S(2)}) async-start(), calls=%async_computation.1 | async-start | bytes 2621440 | tf_op jit(solution)/shard_map/all_gather | solution.py:120
  8.0 665.3 %reduce-scatter.2.cloned.1.call-start = ((), (), s32[]{:S(2)}) async-start(), calls=%async_computation.3 | async-start | bytes 2621440 | tf_op jit(solution)/shard_map/reduce_scatter | solution.py:135
  94.8 10.3 %collective-permute-start = (f32[4,1,7,1024]{3,2,1,0:T(8,128)}, f32[4,1,7,1024]{3,2,1,0:T(8,128)S(1)}, u32[]{:S(2)}, u32[]{:S(2)}) collective-permute-start(f32[4,1,7,1024]{3,2,1,0:T(8,128)} %get-tuple-element.707), channel_id=1, source_target_pairs={{1,0},{2,1},{3,2},{4,3},{5,4},{6,5},{7,6},{9,8},{10,9},{11,10},{12... | collective-permute-start | bytes 344072 | tf_op jit(solution)/shard_map/while/body/eval_jaxpr/ppermute | solution.py:25
  131.3 10.3 %collective-permute-start = (f32[4,1,7,1024]{3,2,1,0:T(8,128)}, f32[4,1,7,1024]{3,2,1,0:T(8,128)S(1)}, u32[]{:S(2)}, u32[]{:S(2)}) collective-permute-start(f32[4,1,7,1024]{3,2,1,0:T(8,128)} %get-tuple-element.707), channel_id=1, source_target_pairs={{1,0},{2,1},{3,2},{4,3},{5,4},{6,5},{7,6},{9,8},{10,9},{11,10},{12... | collective-permute-start | bytes 344072 | tf_op jit(solution)/shard_map/while/body/eval_jaxpr/ppermute | solution.py:25
  132.6 9.9 %collective-permute-start.1 = (f32[4,1,7,1024]{3,2,1,0:T(8,128)S(1)}, f32[4,1,7,1024]{3,2,1,0:T(8,128)S(1)}, u32[]{:S(2)}, u32[]{:S(2)}) collective-permute-start(f32[4,1,7,1024]{3,2,1,0:T(8,128)S(1)} %get-tuple-element.708), channel_id=1, source_target_pairs={{0,1},{1,2},{2,3},{3,4},{4,5},{5,6},{6,7},{8,9},{9,10},{10,11},{11... | collective-permute-start | bytes 344072 | tf_op jit(solution)/shard_map/while/body/eval_jaxpr/ppermute | solution.py:22
  167.8 10.3 %collective-permute-start = (f32[4,1,7,1024]{3,2,1,0:T(8,128)}, f32[4,1,7,1024]{3,2,1,0:T(8,128)S(1)}, u32[]{:S(2)}, u32[]{:S(2)}) collective-permute-start(f32[4,1,7,1024]{3,2,1,0:T(8,128)} %get-tuple-element.707), channel_id=1, source_target_pairs={{1,0},{2,1},{3,2},{4,3},{5,4},{6,5},{7,6},{9,8},{10,9},{11,10},{12... | collective-permute-start | bytes 344072 | tf_op jit(solution)/shard_map/while/body/eval_jaxpr/ppermute | solution.py:25
  169.1 9.9 %collective-permute-start.1 = (f32[4,1,7,1024]{3,2,1,0:T(8,128)S(1)}, f32[4,1,7,1024]{3,2,1,0:T(8,128)S(1)}, u32[]{:S(2)}, u32[]{:S(2)}) collective-permute-start(f32[4,1,7,1024]{3,2,1,0:T(8,128)S(1)} %get-tuple-element.708), channel_id=1, source_target_pairs={{0,1},{1,2},{2,3},{3,4},{4,5},{5,6},{6,7},{8,9},{9,10},{10,11},{11... | collective-permute-start | bytes 344072 | tf_op jit(solution)/shard_map/while/body/eval_jaxpr/ppermute | solution.py:22
  204.3 10.3 %collective-permute-start = (f32[4,1,7,1024]{3,2,1,0:T(8,128)}, f32[4,1,7,1024]{3,2,1,0:T(8,128)S(1)}, u32[]{:S(2)}, u32[]{:S(2)}) collective-permute-start(f32[4,1,7,1024]{3,2,1,0:T(8,128)} %get-tuple-element.707), channel_id=1, source_target_pairs={{1,0},{2,1},{3,2},{4,3},{5,4},{6,5},{7,6},{9,8},{10,9},{11,10},{12... | collective-permute-start | bytes 344072 | tf_op jit(solution)/shard_map/while/body/eval_jaxpr/ppermute | solution.py:25
  205.6 9.9 %collective-permute-start.1 = (f32[4,1,7,1024]{3,2,1,0:T(8,128)S(1)}, f32[4,1,7,1024]{3,2,1,0:T(8,128)S(1)}, u32[]{:S(2)}, u32[]{:S(2)}) collective-permute-start(f32[4,1,7,1024]{3,2,1,0:T(8,128)S(1)} %get-tuple-element.708), channel_id=1, source_target_pairs={{0,1},{1,2},{2,3},{3,4},{4,5},{5,6},{6,7},{8,9},{9,10},{10,11},{11... | collective-permute-start | bytes 344072 | tf_op jit(solution)/shard_map/while/body/eval_jaxpr/ppermute | solution.py:22
  240.8 10.3 %collective-permute-start = (f32[4,1,7,1024]{3,2,1,0:T(8,128)}, f32[4,1,7,1024]{3,2,1,0:T(8,128)S(1)}, u32[]{:S(2)}, u32[]{:S(2)}) collective-permute-start(f32[4,1,7,1024]{3,2,1,0:T(8,128)} %get-tuple-element.707), channel_id=1, source_target_pairs={{1,0},{2,1},{3,2},{4,3},{5,4},{6,5},{7,6},{9,8},{10,9},{11,10},{12... | collective-permute-start | bytes 344072 | tf_op jit(solution)/shard_map/while/body/eval_jaxpr/ppermute | solution.py:25
  242.1 9.9 %collective-permute-start.1 = (f32[4,1,7,1024]{3,2,1,0:T(8,128)S(1)}, f32[4,1,7,1024]{3,2,1,0:T(8,128)S(1)}, u32[]{:S(2)}, u32[]{:S(2)}) collective-permute-start(f32[4,1,7,1024]{3,2,1,0:T(8,128)S(1)} %get-tuple-element.708), channel_id=1, source_target_pairs={{0,1},{1,2},{2,3},{3,4},{4,5},{5,6},{6,7},{8,9},{9,10},{10,11},{11... | collective-permute-start | bytes 344072 | tf_op jit(solution)/shard_map/while/body/eval_jaxpr/ppermute | solution.py:22
  277.3 10.3 %collective-permute-start = (f32[4,1,7,1024]{3,2,1,0:T(8,128)}, f32[4,1,7,1024]{3,2,1,0:T(8,128)S(1)}, u32[]{:S(2)}, u32[]{:S(2)}) collective-permute-start(f32[4,1,7,1024]{3,2,1,0:T(8,128)} %get-tuple-element.707), channel_id=1, source_target_pairs={{1,0},{2,1},{3,2},{4,3},{5,4},{6,5},{7,6},{9,8},{10,9},{11,10},{12... | collective-permute-start | bytes 344072 | tf_op jit(solution)/shard_map/while/body/eval_jaxpr/ppermute | solution.py:25
  278.6 9.9 %collective-permute-start.1 = (f32[4,1,7,1024]{3,2,1,0:T(8,128)S(1)}, f32[4,1,7,1024]{3,2,1,0:T(8,128)S(1)}, u32[]{:S(2)}, u32[]{:S(2)}) collective-permute-start(f32[4,1,7,1024]{3,2,1,0:T(8,128)S(1)} %get-tuple-element.708), channel_id=1, source_target_pairs={{0,1},{1,2},{2,3},{3,4},{4,5},{5,6},{6,7},{8,9},{9,10},{10,11},{11... | collective-permute-start | bytes 344072 | tf_op jit(solution)/shard_map/while/body/eval_jaxpr/ppermute | solution.py:22
  313.8 10.3 %collective-permute-start = (f32[4,1,7,1024]{3,2,1,0:T(8,128)}, f32[4,1,7,1024]{3,2,1,0:T(8,128)S(1)}, u32[]{:S(2)}, u32[]{:S(2)}) collective-permute-start(f32[4,1,7,1024]{3,2,1,0:T(8,128)} %get-tuple-element.707), channel_id=1, source_target_pairs={{1,0},{2,1},{3,2},{4,3},{5,4},{6,5},{7,6},{9,8},{10,9},{11,10},{12... | collective-permute-start | bytes 344072 | tf_op jit(solution)/shard_map/while/body/eval_jaxpr/ppermute | solution.py:25
  315.1 9.9 %collective-permute-start.1 = (f32[4,1,7,1024]{3,2,1,0:T(8,128)S(1)}, f32[4,1,7,1024]{3,2,1,0:T(8,128)S(1)}, u32[]{:S(2)}, u32[]{:S(2)}) collective-permute-start(f32[4,1,7,1024]{3,2,1,0:T(8,128)S(1)} %get-tuple-element.708), channel_id=1, source_target_pairs={{0,1},{1,2},{2,3},{3,4},{4,5},{5,6},{6,7},{8,9},{9,10},{10,11},{11... | collective-permute-start | bytes 344072 | tf_op jit(solution)/shard_map/while/body/eval_jaxpr/ppermute | solution.py:22
  350.3 10.3 %collective-permute-start = (f32[4,1,7,1024]{3,2,1,0:T(8,128)}, f32[4,1,7,1024]{3,2,1,0:T(8,128)S(1)}, u32[]{:S(2)}, u32[]{:S(2)}) collective-permute-start(f32[4,1,7,1024]{3,2,1,0:T(8,128)} %get-tuple-element.707), channel_id=1, source_target_pairs={{1,0},{2,1},{3,2},{4,3},{5,4},{6,5},{7,6},{9,8},{10,9},{11,10},{12... | collective-permute-start | bytes 344072 | tf_op jit(solution)/shard_map/while/body/eval_jaxpr/ppermute | solution.py:25
  351.6 9.9 %collective-permute-start.1 = (f32[4,1,7,1024]{3,2,1,0:T(8,128)S(1)}, f32[4,1,7,1024]{3,2,1,0:T(8,128)S(1)}, u32[]{:S(2)}, u32[]{:S(2)}) collective-permute-start(f32[4,1,7,1024]{3,2,1,0:T(8,128)S(1)} %get-tuple-element.708), channel_id=1, source_target_pairs={{0,1},{1,2},{2,3},{3,4},{4,5},{5,6},{6,7},{8,9},{9,10},{10,11},{11... | collective-permute-start | bytes 344072 | tf_op jit(solution)/shard_map/while/body/eval_jaxpr/ppermute | solution.py:22
  386.8 10.3 %collective-permute-start = (f32[4,1,7,1024]{3,2,1,0:T(8,128)}, f32[4,1,7,1024]{3,2,1,0:T(8,128)S(1)}, u32[]{:S(2)}, u32[]{:S(2)}) collective-permute-start(f32[4,1,7,1024]{3,2,1,0:T(8,128)} %get-tuple-element.707), channel_id=1, source_target_pairs={{1,0},{2,1},{3,2},{4,3},{5,4},{6,5},{7,6},{9,8},{10,9},{11,10},{12... | collective-permute-start | bytes 344072 | tf_op jit(solution)/shard_map/while/body/eval_jaxpr/ppermute | solution.py:25
  388.1 9.9 %collective-permute-start.1 = (f32[4,1,7,1024]{3,2,1,0:T(8,128)S(1)}, f32[4,1,7,1024]{3,2,1,0:T(8,128)S(1)}, u32[]{:S(2)}, u32[]{:S(2)}) collective-permute-start(f32[4,1,7,1024]{3,2,1,0:T(8,128)S(1)} %get-tuple-element.708), channel_id=1, source_target_pairs={{0,1},{1,2},{2,3},{3,4},{4,5},{5,6},{6,7},{8,9},{9,10},{10,11},{11... | collective-permute-start | bytes 344072 | tf_op jit(solution)/shard_map/while/body/eval_jaxpr/ppermute | solution.py:22
  423.3 10.3 %collective-permute-start = (f32[4,1,7,1024]{3,2,1,0:T(8,128)}, f32[4,1,7,1024]{3,2,1,0:T(8,128)S(1)}, u32[]{:S(2)}, u32[]{:S(2)}) collective-permute-start(f32[4,1,7,1024]{3,2,1,0:T(8,128)} %get-tuple-element.707), channel_id=1, source_target_pairs={{1,0},{2,1},{3,2},{4,3},{5,4},{6,5},{7,6},{9,8},{10,9},{11,10},{12... | collective-permute-start | bytes 344072 | tf_op jit(solution)/shard_map/while/body/eval_jaxpr/ppermute | solution.py:25
  424.6 9.9 %collective-permute-start.1 = (f32[4,1,7,1024]{3,2,1,0:T(8,128)S(1)}, f32[4,1,7,1024]{3,2,1,0:T(8,128)S(1)}, u32[]{:S(2)}, u32[]{:S(2)}) collective-permute-start(f32[4,1,7,1024]{3,2,1,0:T(8,128)S(1)} %get-tuple-element.708), channel_id=1, source_target_pairs={{0,1},{1,2},{2,3},{3,4},{4,5},{5,6},{6,7},{8,9},{9,10},{10,11},{11... | collective-permute-start | bytes 344072 | tf_op jit(solution)/shard_map/while/body/eval_jaxpr/ppermute | solution.py:22
  459.8 10.3 %collective-permute-start = (f32[4,1,7,1024]{3,2,1,0:T(8,128)}, f32[4,1,7,1024]{3,2,1,0:T(8,128)S(1)}, u32[]{:S(2)}, u32[]{:S(2)}) collective-permute-start(f32[4,1,7,1024]{3,2,1,0:T(8,128)} %get-tuple-element.707), channel_id=1, source_target_pairs={{1,0},{2,1},{3,2},{4,3},{5,4},{6,5},{7,6},{9,8},{10,9},{11,10},{12... | collective-permute-start | bytes 344072 | tf_op jit(solution)/shard_map/while/body/eval_jaxpr/ppermute | solution.py:25
  461.1 9.9 %collective-permute-start.1 = (f32[4,1,7,1024]{3,2,1,0:T(8,128)S(1)}, f32[4,1,7,1024]{3,2,1,0:T(8,128)S(1)}, u32[]{:S(2)}, u32[]{:S(2)}) collective-permute-start(f32[4,1,7,1024]{3,2,1,0:T(8,128)S(1)} %get-tuple-element.708), channel_id=1, source_target_pairs={{0,1},{1,2},{2,3},{3,4},{4,5},{5,6},{6,7},{8,9},{9,10},{10,11},{11... | collective-permute-start | bytes 344072 | tf_op jit(solution)/shard_map/while/body/eval_jaxpr/ppermute | solution.py:22
  496.3 10.3 %collective-permute-start = (f32[4,1,7,1024]{3,2,1,0:T(8,128)}, f32[4,1,7,1024]{3,2,1,0:T(8,128)S(1)}, u32[]{:S(2)}, u32[]{:S(2)}) collective-permute-start(f32[4,1,7,1024]{3,2,1,0:T(8,128)} %get-tuple-element.707), channel_id=1, source_target_pairs={{1,0},{2,1},{3,2},{4,3},{5,4},{6,5},{7,6},{9,8},{10,9},{11,10},{12... | collective-permute-start | bytes 344072 | tf_op jit(solution)/shard_map/while/body/eval_jaxpr/ppermute | solution.py:25
  497.6 9.9 %collective-permute-start.1 = (f32[4,1,7,1024]{3,2,1,0:T(8,128)S(1)}, f32[4,1,7,1024]{3,2,1,0:T(8,128)S(1)}, u32[]{:S(2)}, u32[]{:S(2)}) collective-permute-start(f32[4,1,7,1024]{3,2,1,0:T(8,128)S(1)} %get-tuple-element.708), channel_id=1, source_target_pairs={{0,1},{1,2},{2,3},{3,4},{4,5},{5,6},{6,7},{8,9},{9,10},{10,11},{11... | collective-permute-start | bytes 344072 | tf_op jit(solution)/shard_map/while/body/eval_jaxpr/ppermute | solution.py:22
  532.8 10.3 %collective-permute-start = (f32[4,1,7,1024]{3,2,1,0:T(8,128)}, f32[4,1,7,1024]{3,2,1,0:T(8,128)S(1)}, u32[]{:S(2)}, u32[]{:S(2)}) collective-permute-start(f32[4,1,7,1024]{3,2,1,0:T(8,128)} %get-tuple-element.707), channel_id=1, source_target_pairs={{1,0},{2,1},{3,2},{4,3},{5,4},{6,5},{7,6},{9,8},{10,9},{11,10},{12... | collective-permute-start | bytes 344072 | tf_op jit(solution)/shard_map/while/body/eval_jaxpr/ppermute | solution.py:25
  534.1 9.9 %collective-permute-start.1 = (f32[4,1,7,1024]{3,2,1,0:T(8,128)S(1)}, f32[4,1,7,1024]{3,2,1,0:T(8,128)S(1)}, u32[]{:S(2)}, u32[]{:S(2)}) collective-permute-start(f32[4,1,7,1024]{3,2,1,0:T(8,128)S(1)} %get-tuple-element.708), channel_id=1, source_target_pairs={{0,1},{1,2},{2,3},{3,4},{4,5},{5,6},{6,7},{8,9},{9,10},{10,11},{11... | collective-permute-start | bytes 344072 | tf_op jit(solution)/shard_map/while/body/eval_jaxpr/ppermute | solution.py:22
  569.3 10.3 %collective-permute-start = (f32[4,1,7,1024]{3,2,1,0:T(8,128)}, f32[4,1,7,1024]{3,2,1,0:T(8,128)S(1)}, u32[]{:S(2)}, u32[]{:S(2)}) collective-permute-start(f32[4,1,7,1024]{3,2,1,0:T(8,128)} %get-tuple-element.707), channel_id=1, source_target_pairs={{1,0},{2,1},{3,2},{4,3},{5,4},{6,5},{7,6},{9,8},{10,9},{11,10},{12... | collective-permute-start | bytes 344072 | tf_op jit(solution)/shard_map/while/body/eval_jaxpr/ppermute | solution.py:25
  570.6 9.9 %collective-permute-start.1 = (f32[4,1,7,1024]{3,2,1,0:T(8,128)S(1)}, f32[4,1,7,1024]{3,2,1,0:T(8,128)S(1)}, u32[]{:S(2)}, u32[]{:S(2)}) collective-permute-start(f32[4,1,7,1024]{3,2,1,0:T(8,128)S(1)} %get-tuple-element.708), channel_id=1, source_target_pairs={{0,1},{1,2},{2,3},{3,4},{4,5},{5,6},{6,7},{8,9},{9,10},{10,11},{11... | collective-permute-start | bytes 344072 | tf_op jit(solution)/shard_map/while/body/eval_jaxpr/ppermute | solution.py:22
  605.8 10.3 %collective-permute-start = (f32[4,1,7,1024]{3,2,1,0:T(8,128)}, f32[4,1,7,1024]{3,2,1,0:T(8,128)S(1)}, u32[]{:S(2)}, u32[]{:S(2)}) collective-permute-start(f32[4,1,7,1024]{3,2,1,0:T(8,128)} %get-tuple-element.707), channel_id=1, source_target_pairs={{1,0},{2,1},{3,2},{4,3},{5,4},{6,5},{7,6},{9,8},{10,9},{11,10},{12... | collective-permute-start | bytes 344072 | tf_op jit(solution)/shard_map/while/body/eval_jaxpr/ppermute | solution.py:25
  607.0 9.9 %collective-permute-start.1 = (f32[4,1,7,1024]{3,2,1,0:T(8,128)S(1)}, f32[4,1,7,1024]{3,2,1,0:T(8,128)S(1)}, u32[]{:S(2)}, u32[]{:S(2)}) collective-permute-start(f32[4,1,7,1024]{3,2,1,0:T(8,128)S(1)} %get-tuple-element.708), channel_id=1, source_target_pairs={{0,1},{1,2},{2,3},{3,4},{4,5},{5,6},{6,7},{8,9},{9,10},{10,11},{11... | collective-permute-start | bytes 344072 | tf_op jit(solution)/shard_map/while/body/eval_jaxpr/ppermute | solution.py:22
  (499 other events, 399.4 us)
Sparse Core Ops, SparseCore 0:
  8.9 25.2 all-gather.4
  35.8 22.5 all-gather.2
  641.7 31.4 reduce-scatter.1
where the time goes:
time: 684 us; the launch traced here: 682 us
  other arithmetic  388 us (57%)
  starting transfers between devices  100 us (15%)
  waiting for transfers between devices  91.6 us (13%)
  local copies, waits for them, and re-layouts  81.6 us (12%)
  between operations  13.2 us (2%)
  loops' own time  7.26 us (1%)
    reduce_sum x16, other arithmetic, advance(): jnp.sum(weights * phased_re, axis=0)  255 us
    ppermute x16, starting transfers between devices, padded_2(): lax.ppermute(lax.slice_in_dim(block, block.shape[dim] - width, None, axis...  79.9 us
    add x32, other arithmetic, convolve_rows(): out_im = out_im + coef_re * part_im + coef_im * part_re  48.5 us
    sub x32, other arithmetic, convolve_rows(): out_re = out_re + coef_re * part_re - coef_im * part_im  48.3 us
    mul x80, local copies, waits for them, and re-layouts, convolve_rows(): out_re = out_re + coef_re * part_re - coef_im * part_im  39.6 us
    reduce_scatter x1, waiting for transfers between devices, local(): lax.psum_scatter(jnp.sum(pieces, axis=1), 'depth', scatter_dimension=0, t...  31.7 us
    all_gather x1, waiting for transfers between devices, local(): lax.all_gather(zone_index, 'depth', axis=0, tiled=True)  22.4 us
    all_gather x1, waiting for transfers between devices, local(): lax.all_gather(blend_weight, 'depth', axis=0, tiled=True)  21.4 us
  transfers between devices with their start and end apart: 35, of which 19 were waited for; matrix products, arithmetic and copies ran while one was open for 10% of the time, Pallas kernels for 0%

commit v1 on v0

v1 whole, which is shorter than its diff:
```python
import functools
import math

import jax
import jax.numpy as jnp
from jax import lax
from jax.experimental import pallas as pl
from jax.experimental.pallas import tpu as pltpu
from jax.sharding import PartitionSpec as P

HALF = 7
BLEND = 16
TAPS = 2 * HALF + 1
SPAN = 2 * HALF
LANES = 128
WIN = LANES - SPAN
BLK = 16
AXES = ("depth", "lat")
OFF = 8

cell_width = 5.0
depth_step = 10.0
taper_width = 16.0

f32 = jnp.float32
bf16 = jnp.bfloat16


def cdiv(a, b):
    return -(-a // b)


def kernels(frequencies, ref_velocity):
    offsets = jnp.arange(-HALF, HALF + 1, dtype=jnp.int32).astype(jnp.float32)
    wavenumber = 2.0 * math.pi * frequencies.astype(jnp.float32)[:, None] / ref_velocity[None, :]
    curvature = wavenumber * (cell_width * cell_width / (2.0 * depth_step))
    phase_turn = wavenumber * depth_step
    chirp_angle = curvature[:, :, None] * (offsets * offsets)[None, None, :]
    envelope = jnp.exp(-offsets * offsets / taper_width)
    raw_re = envelope * jnp.cos(chirp_angle)
    raw_im = envelope * jnp.sin(chirp_angle)
    magnitude = jnp.sqrt(jnp.sum(raw_re, axis=-1) ** 2 + jnp.sum(raw_im, axis=-1) ** 2)[:, :, None]
    return (raw_re / magnitude, raw_im / magnitude, jnp.cos(phase_turn), jnp.sin(phase_turn))


def halves(x):
    high = lax.reduce_precision(x, 8, 7)
    return high.astype(bf16), (x - high).astype(bf16)


def operators(tap_re, tap_im, turn_cos, turn_sin):
    def band(taps, index, valid):
        out = jnp.zeros(taps.shape[:-1] + index.shape, f32)
        for m in range(TAPS):
            out = out + jnp.where((index == m) & valid, taps[..., m][..., None, None], 0.0)
        return out

    count, refs = tap_re.shape[:2]
    index = jnp.arange(2 * BLK)[None, :] - jnp.arange(BLK)[:, None]
    re, im = band(tap_re, index, True), band(tap_im, index, True)
    rows = jnp.stack([jnp.concatenate([re, -im], -1), jnp.concatenate([im, re], -1)], 2)
    high, low = halves(rows.reshape(count, refs * 2 * BLK, 4 * BLK))
    by_rows = jnp.concatenate([high, high, low], -1)
    ph_re = tap_re * turn_cos[..., None] - tap_im * turn_sin[..., None]
    ph_im = tap_re * turn_sin[..., None] + tap_im * turn_cos[..., None]
    column = jnp.arange(LANES)[None, :]
    index = jnp.arange(LANES)[:, None] - column
    re, im = band(ph_re, index, column < WIN), band(ph_im, index, column < WIN)
    cols = jnp.concatenate(
        [jnp.concatenate([re, im], -1), jnp.concatenate([-im, re], -1)], -2
    )
    high, low = halves(cols)
    by_cols = jnp.concatenate([high, high, low], -2)
    return by_rows, by_cols


def split(v):
    high = v.astype(bf16)
    return high, (v - high.astype(f32)).astype(bf16)


def window(x, start, b):
    low = start + WIN * b
    high = min(low + LANES, x.shape[1])
    part = x[:, low:high]
    if high - low < LANES:
        part = jnp.concatenate(
            [part, jnp.zeros((x.shape[0], LANES - (high - low)), x.dtype)], axis=1
        )
    return part


def dense(get, start, count):
    pieces = []
    n = start
    while n < start + count:
        b = n // WIN
        end = min(WIN * (b + 1), start + count)
        pieces.append(get(b)[:, n - WIN * b : end - WIN * b])
        n = end
    return jnp.concatenate(pieces, axis=1)


def stage_kernel(
    levels, rows, cols, windows, blocks, refs,
    tile_ref, t_ref, a_ref, c_ref, out_ref, img_ref, cur_ref, y_ref, tw_ref, im_ref,
):
    height = tile_ref.shape[1]
    held = cur_ref.shape[2]
    each = 2 * windows
    lanes = windows * LANES
    for l in range(levels):
        h = height - SPAN * (l + 1)
        x = t_ref[l, HALF * l : HALF * l + h, :]
        for b in range(windows):
            tw_ref[l, 0:h, b * LANES : (b + 1) * LANES] = window(x, HALF * l, b)
        tw_ref[l, h:held, :] = jnp.full((held - h, lanes), -8.0, f32)
    for f in range(2):
        for p in range(2):
            x = tile_ref[2 * f + p]
            for b in range(windows):
                high, low = split(window(x, 0, b))
                at = (f * windows + b) * LANES
                cur_ref[p, 0, 0:height, at : at + LANES] = high
                cur_ref[p, 1, 0:height, at : at + LANES] = low
    if held > height:
        cur_ref[:, :, height:held, :] = jnp.zeros((2, 2, held - height, 2 * lanes), bf16)
    lane = lax.broadcasted_iota(jnp.int32, (BLK, LANES), 1)

    def chunk(l, i, carry):
        base = pl.multiple_of(i * (BLK * blocks), BLK * blocks)
        for k in range(blocks):
            r = pl.ds(pl.multiple_of(base + BLK * k, BLK), 2 * BLK)
            rhi, rlo = cur_ref[0, 0, r, :], cur_ref[0, 1, r, :]
            ihi, ilo = cur_ref[1, 0, r, :], cur_ref[1, 1, r, :]
            rhs = jnp.concatenate([rhi, ihi, rlo, ilo, rhi, ihi], axis=0)
            g = jnp.dot(a_ref[...], rhs, preferred_element_type=f32)
            high, low = split(g)
            for j in range(refs):
                for p in range(2):
                    s = (2 * j + p) * BLK
                    for q in range(each):
                        rr = (k * each + q) * BLK
                        at = q * LANES
                        y_ref[j, rr : rr + BLK, p * LANES : (p + 1) * LANES] = high[
                            s : s + BLK, at : at + LANES
                        ]
                        y_ref[j, rr : rr + BLK, (2 + p) * LANES : (3 + p) * LANES] = low[
                            s : s + BLK, at : at + LANES
                        ]
        t = tw_ref[l, pl.ds(base, BLK * blocks), :]
        acc = None
        for j in range(refs):
            y = y_ref[j]
            full = jnp.dot(
                jnp.concatenate([y, y[:, : 2 * LANES]], axis=1),
                c_ref[j],
                preferred_element_type=f32,
            )
            w = jnp.maximum(1.0 - jnp.abs(t - float(j)), 0.0)
            new = []
            for k in range(blocks):
                for f in range(2):
                    for b in range(windows):
                        rr = (k * each + f * windows + b) * BLK
                        wk = w[BLK * k : BLK * (k + 1), b * LANES : (b + 1) * LANES]
                        new.append(
                            (wk * full[rr : rr + BLK, :LANES], wk * full[rr : rr + BLK, LANES:])
                        )
            if acc is None:
                acc = new
            else:
                acc = [(a0 + b0, a1 + b1) for (a0, a1), (b0, b1) in zip(acc, new)]
        for k in range(blocks):
            r = pl.ds(pl.multiple_of(base + BLK * k, BLK), BLK)
            for b in range(windows):
                s = acc[k * each + b]
                q = acc[k * each + windows + b]
                im_ref[l, r, b * LANES : (b + 1) * LANES] = s[0] * q[0] - s[1] * q[1]
            for f in range(2):
                for b in range(windows):
                    at = (f * windows + b) * LANES
                    for p in range(2):
                        v = acc[k * each + f * windows + b][p]
                        if b + 1 < windows:
                            after = pltpu.roll(acc[k * each + f * windows + b + 1][p], WIN, 1)
                            v = jnp.where(lane < WIN, v, after)
                        high, low = split(v)
                        cur_ref[p, 0, r, at : at + LANES] = high
                        cur_ref[p, 1, r, at : at + LANES] = low
        return carry

    def level(l, carry):
        count = (height - SPAN * (l + 1) + BLK * blocks - 1) // (BLK * blocks)
        return lax.fori_loop(0, count, functools.partial(chunk, l), carry)

    lax.fori_loop(0, levels, level, 0)
    for f in range(2):
        for p in range(2):

            def get(b):
                at = (f * windows + b) * LANES
                return cur_ref[p, 0, 0:rows, at : at + LANES].astype(f32) + cur_ref[
                    p, 1, 0:rows, at : at + LANES
                ].astype(f32)

            out_ref[2 * f + p] = dense(get, 0, cols)
    for l in range(levels):
        o = HALF * (levels - 1 - l)
        img_ref[l] = dense(
            lambda b: im_ref[l, o : o + rows, b * LANES : (b + 1) * LANES], o, cols
        )


def stage(tile, t, by_rows, by_cols, rows, cols, blocks=4):
    levels = t.shape[0]
    height = tile.shape[1]
    refs = by_cols.shape[0]
    windows = cdiv(cols + SPAN * (levels - 1), WIN)
    step = BLK * blocks
    held = max(cdiv(height - SPAN, step) * step + BLK, cdiv(height, BLK) * BLK)
    body = functools.partial(stage_kernel, levels, rows, cols, windows, blocks, refs)
    area = levels * (height + rows) // 2 * windows * LANES
    return pl.pallas_call(
        body,
        out_shape=[
            jax.ShapeDtypeStruct((4, rows, cols), f32),
            jax.ShapeDtypeStruct((levels, rows, cols), f32),
        ],
        scratch_shapes=[
            pltpu.VMEM((2, 2, held, 2 * windows * LANES), bf16),
            pltpu.VMEM((refs, blocks * 2 * windows * BLK, 4 * LANES), bf16),
            pltpu.VMEM((levels, held, windows * LANES), f32),
            pltpu.VMEM((levels, held, windows * LANES), f32),
        ],
        compiler_params=pltpu.CompilerParams(vmem_limit_bytes=40 * 2**20),
        cost_estimate=pl.CostEstimate(
            flops=area * 2 * refs * 2 * 3 * 512, bytes_accessed=4 * tile.size, transcendentals=0
        ),
    )(tile, t, by_rows, by_cols)


def local(source_field, receiver_field, zone_index, blend_weight, ref_velocity, frequencies):
    depth, lat = lax.axis_size("depth"), lax.axis_size("lat")
    d, l = lax.axis_index("depth"), lax.axis_index("lat")
    hi, core = d // 2, d % 2
    pair, side = l // 2, l % 2
    if depth != 4 or lat % 2:
        raise ValueError("mesh")
    levels, strip, width = zone_index.shape
    freq_count = source_field.shape[1]
    per_core = freq_count // 2
    rows, cols = 2 * strip, width // 4
    halo = HALF * levels
    edge = halo - HALF

    def permutation(move):
        out = []
        for i in range(depth * lat):
            dd, ll = divmod(i, lat)
            target = move(dd // 2, dd % 2, ll // 2, ll % 2)
            if target is None:
                continue
            h2, c2, p2, s2 = target
            if 0 <= p2 < lat // 2:
                out.append((i, (h2 * 2 + c2) * lat + p2 * 2 + s2))
        return out

    across_hi = permutation(lambda h, c, p, s: (1 - h, c, p, s))
    across_side = permutation(lambda h, c, p, s: (h, c, p, 1 - s))
    across_both = permutation(lambda h, c, p, s: (1 - h, c, p, 1 - s))
    across_core = permutation(lambda h, c, p, s: (h, 1 - c, p, s))
    pairs_even = permutation(lambda h, c, p, s: (h, c, p + 1 - 2 * (p % 2), s))
    pairs_odd = permutation(lambda h, c, p, s: (h, c, p - 1 + 2 * (p % 2), s))
    middle = permutation(lambda h, c, p, s: (1 - h, c, p, s) if s == 1 else None)

    def move(x, pairs):
        return lax.ppermute(x, AXES, pairs)

    def place(h, s):
        return 2 * h + jnp.where(h == 0, s, 1 - s)

    block = place(hi, side)

    def exchange_rows(x, count, axis):
        size = x.shape[axis]
        top = lax.slice_in_dim(x, 0, count, axis=axis)
        bottom = lax.slice_in_dim(x, size - count, size, axis=axis)
        even = pair % 2 == 0
        got_a = move(jnp.where(even, bottom, top), pairs_even)
        got_b = move(jnp.where(even, top, bottom), pairs_odd)
        return jnp.where(even, got_b, got_a), jnp.where(even, got_a, got_b)

    def exchange_cols(x, count):
        even = block % 2 == 0
        left, right = x[..., :count], x[..., -count:]
        got_a = move(jnp.where(even, right, left), across_side)
        got_b = move(jnp.where(even, left, right), middle)
        return jnp.where(even, got_b, got_a), jnp.where(even, got_a, got_b)

    def columns(x, which, size):
        return lax.dynamic_slice_in_dim(x, which * cols, size, x.ndim - 1)

    def by_side(mine, other, axis):
        return jnp.concatenate(
            [jnp.where(side == 0, mine, other), jnp.where(side == 0, other, mine)], axis=axis
        )

    tables = jnp.stack([zone_index + OFF, blend_weight])
    tables = jnp.pad(tables, ((0, 0),) * 3 + ((edge, edge),))
    size = cols + 2 * edge
    mine = columns(tables, block, size)
    got_hi = move(columns(tables, place(1 - hi, side), size), across_hi)
    got_side = move(columns(tables, place(hi, 1 - side), size), across_side)
    got_both = move(columns(tables, place(1 - hi, 1 - side), size), across_both)
    stage_t = [None] * 4
    for s in range(2):
        whole = by_side(
            jnp.where(hi == s, mine, got_hi), jnp.where(hi == s, got_side, got_both), 2
        )
        above, below = exchange_rows(whole, edge, 2)
        whole = jnp.concatenate([above, whole, below], axis=2)
        other = move(whole, across_core)
        for k in range(2):
            pick = jnp.where(core == k, whole, other)
            stage_t[2 * s + k] = (pick[0] - OFF).astype(f32) + pick[1].astype(f32) / BLEND

    surface = jnp.stack(
        [source_field[0], source_field[1], receiver_field[0], -receiver_field[1]], axis=1
    )
    surface = lax.dynamic_slice_in_dim(surface, core * per_core, per_core, 0)
    surface = jnp.pad(surface, ((0, 0),) * 3 + ((halo, halo),))
    size = cols + 2 * halo
    tiles = []
    for q in range(per_core):
        mine = columns(surface[q], block, size)
        other = move(columns(surface[q], place(hi, 1 - side), size), across_side)
        tile = by_side(mine, other, 1)
        above, below = exchange_rows(tile, halo, 1)
        tiles.append(jnp.concatenate([above, tile, below], axis=1))

    tap_re, tap_im, turn_cos, turn_sin = kernels(frequencies, ref_velocity)
    by_rows, by_cols = operators(tap_re, tap_im, turn_cos, turn_sin)
    by_rows = lax.dynamic_slice_in_dim(by_rows, core * per_core, per_core, 0)
    by_cols = lax.dynamic_slice_in_dim(by_cols, core * per_core, per_core, 0)

    images = []
    for s in range(4):
        image = None
        for q in range(per_core):
            field, part = stage(tiles[q], stage_t[s], by_rows[q], by_cols[q], rows, cols)
            image = part if image is None else image + part
            if s < 3:
                above, below = exchange_rows(field, halo, 1)
                field = jnp.concatenate([above, field, below], axis=1)
                left, right = exchange_cols(field, halo)
                tiles[q] = jnp.concatenate([left, field, right], axis=2)
        images.append(image)

    sums = []
    for s in range(2):
        mine = jnp.where(core == 0, images[2 * s], images[2 * s + 1])
        other = jnp.where(core == 0, images[2 * s + 1], images[2 * s])
        sums.append(mine + move(other, across_core))
    here = jnp.where(hi == 0, sums[0], sums[1])
    there = jnp.where(hi == 0, sums[1], sums[0])

    def strip_of(x, s):
        return lax.dynamic_slice_in_dim(x, s * strip, strip, 1)

    mine = strip_of(here, side)
    got_hi = move(strip_of(there, side), across_hi)
    got_side = move(strip_of(here, 1 - side), across_side)
    got_both = move(strip_of(there, 1 - side), across_both)
    pieces = []
    for k in range(4):
        piece = jnp.where(
            block == k,
            mine,
            jnp.where(
                place(1 - hi, side) == k,
                got_hi,
                jnp.where(place(hi, 1 - side) == k, got_side, got_both),
            ),
        )
        pieces.append(piece)
    return jnp.concatenate(pieces, axis=2) * (1.0 / freq_count)


def solution(mesh):
    in_specs = (
        P(None, None, "lat", None),
        P(None, None, "lat", None),
        P("depth", "lat", None),
        P("depth", "lat", None),
        P(),
        P(),
    )
    out_specs = P("depth", "lat", None)
    return jax.shard_map(local, mesh=mesh, in_specs=in_specs, out_specs=out_specs, check_vma=False)
```

time: 684 us -> 242 us (0.35)
  other arithmetic: 388 us -> 37.1 us
  Pallas kernels: 0 us -> 71.7 us
  local copies, waits for them, and re-layouts: 81.6 us -> 19.3 us
  waiting for transfers between devices: 91.6 us -> 36.2 us
  starting transfers between devices: 100 us -> 75.2 us
  between operations: 13.2 us -> 1.16 us
  loops' own time: 7.26 us -> 0 us
    reduce_sum x16 -> x0, other arithmetic: 255 us -> none  [advance(): jnp.sum(weights * phased_re, axis=0)]
    pallas_call x0 -> x8, Pallas kernels: none -> 71.7 us  [stage(): pl.pallas_call(body, out_shape=[jax.ShapeDtypeStruct((4, rows, cols), f32...]
    sub x32 -> x0, other arithmetic: 48.3 us -> none  [convolve_rows(): out_re = out_re + coef_re * part_re - coef_im * part_im]
    add x32 -> x5, other arithmetic: 48.5 us -> 3.27 us  [the longest x2 2.51 us: band(): out + jnp.where((index == m) & valid, taps[..., m][..., None, None], 0.0)]
    all_gather x2 -> x0, waiting for transfers between devices: 43.8 us -> none  [the longest x1 22.4 us: local(): lax.all_gather(zone_index, 'depth', axis=0, tiled=True)]
    mul x80 -> x0, local copies, waits for them, and re-layouts: 39.6 us -> none  [convolve_rows(): out_re = out_re + coef_re * part_re - coef_im * part_im]
    slice x48 -> x1, local copies, waits for them, and re-layouts: 32.7 us -> 0.37 us  [local(): mine = columns(surface[q], block, size)]
    reduce_scatter x1 -> x0, waiting for transfers between devices: 31.7 us -> none  [local(): lax.psum_scatter(jnp.sum(pieces, axis=1), 'depth', scatter_dimension=0, t...]
  transfers between devices with their start and end apart: 35 -> 44, of which waited for: 19 -> 11; matrix products, arithmetic and copies ran while one was open for 10% -> 17% of each run, Pallas kernels for 0% -> 26%
where the time goes in v1:
time: 242 us; the launch traced here: 241 us
  starting transfers between devices  75.2 us (31%)
  Pallas kernels  71.7 us (30%)
  other arithmetic  37.1 us (15%)
  waiting for transfers between devices  36.2 us (15%)
  local copies, waits for them, and re-layouts  19.3 us (8%)
    ppermute x44, starting transfers between devices, move(): return lax.ppermute(x, AXES, pairs)  75.2 us
    pallas_call x8, Pallas kernels, stage(): pl.pallas_call(body, out_shape=[jax.ShapeDtypeStruct((4, rows, cols), f32...  71.7 us
    ppermute x44, waiting for transfers between devices, move(): return lax.ppermute(x, AXES, pairs)  36.2 us
    select_n x2, other arithmetic, local(): pick = jnp.where(core == k, whole, other)  5.59 us
    unnamed x76, local copies, waits for them, and re-layouts  5.54 us
    ppermute x2, local copies, waits for them, and re-layouts, move(): return lax.ppermute(x, AXES, pairs)  5.06 us
    concatenate x2, local copies, waits for them, and re-layouts, local(): whole = jnp.concatenate([above, whole, below], axis=2)  5.01 us
  transfers between devices with their start and end apart: 44, of which 11 were waited for; matrix products, arithmetic and copies ran while one was open for 17% of the time, Pallas kernels for 26%

profile of v1, /device:TPU:0, one launch (start us, length us, event | category | flops | bytes accessed | tf_op | source)
XLA Modules:
  0.0 240.6 jit_solution(13542355386140197691)
XLA Ops:
  3.7 2.9 %collective-permute-start.3 = (s32[2,4,32,298]{3,2,1,0:T(8,128)}, s32[2,4,32,298]{3,2,1,0:T(8,128)}, u32[]{:S(2)}, u32[]{:S(2)}) collective-permute-start(s32[2,4,32,298]{3,2,1,0:T(8,128)} %get-tuple-element.56), channel_id=1, source_target_pairs={{0,16},{1,17},{2,18},{3,19},{4,20},{5,21},{6,22},{7,23},{8,24},{9,... | collective-permute-start | bytes 915464 | tf_op jit(solution)/shard_map/ppermute | solution.py:278
  17.7 2.2 fusion.80
  21.4 12.9 %collective-permute-done.9 = f32[4,32,312]{2,1,0:T(8,128)} collective-permute-done((f32[4,32,312]{2,1,0:T(8,128)}, f32[4,32,312]{2,1,0:T(8,128)}, u32[]{:S(2)}, u32[]{:S(2)}) %collective-permute-start.9) | collective-permute-done | bytes 159776 | tf_op jit(solution)/shard_map/ppermute | solution.py:278
  37.7 3.8 %collective-permute-start.11 = (f32[4,28,312]{2,1,0:T(8,128)}, f32[4,28,312]{2,1,0:T(8,128)}, u32[]{:S(2)}, u32[]{:S(2)}) collective-permute-start(f32[4,28,312]{2,1,0:T(8,128)} %get-tuple-element.106), channel_id=1, source_target_pairs={{0,2},{1,3},{2,0},{3,1},{4,6},{5,7},{6,4},{7,5},{8,10},{9,11},{10,... | collective-permute-start | bytes 419336 | tf_op jit(solution)/shard_map/ppermute | solution.py:278
  47.4 3.9 %collective-permute-start.7 = (s32[2,4,21,298]{3,2,1,0:T(8,128)S(1)}, s32[2,4,21,298]{3,2,1,0:T(8,128)S(1)}, u32[]{:S(2)}, u32[]{:S(2)}) collective-permute-start(s32[2,4,21,298]{3,2,1,0:T(8,128)S(1)} %get-tuple-element.68), channel_id=1, source_target_pairs={{0,2},{1,3},{2,0},{3,1},{4,6},{5,7},{6,4},{7,5},{8,10},{9,11},{10,... | collective-permute-start | bytes 600776 | tf_op jit(solution)/shard_map/ppermute | solution.py:278
  53.6 2.7 %collective-permute-done.7 = s32[2,4,21,298]{3,2,1,0:T(8,128)S(1)} collective-permute-done((s32[2,4,21,298]{3,2,1,0:T(8,128)S(1)}, s32[2,4,21,298]{3,2,1,0:T(8,128)S(1)}, u32[]{:S(2)}, u32[]{:S(2)}) %collective-permute-start.7) | collective-permute-done | bytes 200288 | tf_op jit(solution)/shard_map/ppermute | solution.py:278
  56.3 4.4 %collective-permute-start.26 = (s32[2,4,21,298]{3,2,1,0:T(8,128)}, s32[2,4,21,298]{3,2,1,0:T(8,128)}, u32[]{:S(2)}, u32[]{:S(2)}) collective-permute-start(s32[2,4,21,298]{3,2,1,0:T(8,128)} %get-tuple-element.64), channel_id=1, source_target_pairs={{0,2},{1,3},{2,0},{3,1},{4,6},{5,7},{6,4},{7,5},{8,10},{9,11},{10,... | collective-permute-start | bytes 600776 | tf_op jit(solution)/shard_map/ppermute | solution.py:278
  62.9 2.5 %copy.8 = s32[2,4,106,298]{2,1,3,0:T(4,128)} copy(s32[2,4,106,298]{3,2,1,0:T(8,128)} %pad_add_fusion) | data formatting | bytes 2021632 | tf_op jit(solution)/shard_map/concatenate | solution.py:322
  70.1 2.5 %copy.12 = s32[2,4,106,298]{2,1,3,0:T(4,128)} copy(s32[2,4,106,298]{3,2,1,0:T(8,128)} %pad_add_fusion.1) | data formatting | bytes 2021632 | tf_op jit(solution)/shard_map/concatenate | solution.py:322
  78.2 2.5 %copy.9 = s32[2,4,106,298]{3,2,1,0:T(8,128)} copy(s32[2,4,106,298]{2,1,3,0:T(4,128)} %collective-permute-done.8) | data formatting | bytes 2021632 | tf_op jit(solution)/shard_map/ppermute | solution.py:278
  80.8 3.5 %broadcast_select_fusion.1 = (s32[2,4,106,298]{3,2,1,0:T(8,128)}, s32[2,4,106,298]{3,2,1,0:T(8,128)}) fusion(s32[2,4,106,298]{3,2,1,0:T(8,128)} %copy.9, pred[]{:T(512)S(6)} %eq.340, s32[2,4,21,298]{3,2,1,0:T(8,128)} %copy-done.23, s32[2,4,32,298]{3,2,1,0:T(8,128)} %copy-done.18, s32[2,4,32,298]{3,2,1,0:T(8,128)} %copy-done.19, ...), kind=kLoop, calls=%fused_computation.62 | loop fusion | flops 1263520 | bytes 4043266 | tf_op jit(solution)/shard_map/jit(_where)/select_n | solution.py:325
  84.3 2.5 %copy.13 = s32[2,4,106,298]{3,2,1,0:T(8,128)} copy(s32[2,4,106,298]{2,1,3,0:T(4,128)} %collective-permute-done.27) | data formatting | bytes 2021632 | tf_op jit(solution)/shard_map/ppermute | solution.py:278
  90.5 8.8 %shard_map.65 = (f32[4,64,256]{2,1,0:T(8,128)S(1)}, f32[4,64,256]{2,1,0:T(8,128)S(1)}) custom-call(f32[4,120,312]{2,1,0:T(8,128)S(1)} %copy-done.10, f32[4,106,298]{2,1,0:T(8,128)S(1)} %get-tuple-element.228.t_ref, bf16[128,192]{1,0:T(8,128)(2,1)S(1)} %get-tuple-element.139.a_ref, bf16[4,768,256]{2,1,0:T(8,128)(2,1)S(1)} %get-tuple-element.42.c_ref), custom_call_target="tpu_custom_call" | custom-call | flops 3472883712 | bytes 599040 | tf_op jit(solution)/shard_map/pallas_call | solution.py:224
  100.0 5.1 %collective-permute-start.17 = (f32[4,28,256]{2,1,0:T(8,128)S(1)}, f32[4,28,256]{2,1,0:T(8,128)S(1)}, u32[]{:S(2)}, u32[]{:S(2)}) collective-permute-start(f32[4,28,256]{2,1,0:T(8,128)S(1)} %get-tuple-element.132), channel_id=1, source_target_pairs={{0,2},{1,3},{2,0},{3,1},{4,6},{5,7},{6,4},{7,5},{8,10},{9,11},{10,... | collective-permute-start | bytes 344072 | tf_op jit(solution)/shard_map/ppermute | solution.py:278
  105.1 8.8 %shard_map.64 = (f32[4,64,256]{2,1,0:T(8,128)S(1)}, f32[4,64,256]{2,1,0:T(8,128)S(1)}) custom-call(f32[4,120,312]{2,1,0:T(8,128)S(1)} %copy-done.11, f32[4,106,298]{2,1,0:T(8,128)S(1)} %get-tuple-element.228.t_ref, bf16[128,192]{1,0:T(8,128)(2,1)S(1)} %get-tuple-element.140.a_ref, bf16[4,768,256]{2,1,0:T(8,128)(2,1)S(1)} %get-tuple-element.43.c_ref), custom_call_target="tpu_custom_call" | custom-call | flops 3472883712 | bytes 599040 | tf_op jit(solution)/shard_map/pallas_call | solution.py:224
  117.0 3.0 %collective-permute-done.13 = f32[4,28,256]{2,1,0:T(8,128)S(1)} collective-permute-done((f32[4,28,256]{2,1,0:T(8,128)S(1)}, f32[4,28,256]{2,1,0:T(8,128)S(1)}, u32[]{:S(2)}, u32[]{:S(2)}) %collective-permute-start.13) | collective-permute-done | bytes 114720 | tf_op jit(solution)/shard_map/ppermute | solution.py:278
  120.8 3.4 %collective-permute-start.15 = (f32[4,120,28]{2,1,0:T(8,128)S(1)}, f32[4,120,28]{2,1,0:T(8,128)S(1)}, u32[]{:S(2)}, u32[]{:S(2)}) collective-permute-start(f32[4,120,28]{2,1,0:T(8,128)S(1)} %get-tuple-element.102), channel_id=1, source_target_pairs={{0,1},{1,0},{2,3},{3,2},{4,5},{5,4},{6,7},{7,6},{8,9},{9,8},{10,11... | collective-permute-start | bytes 161288 | tf_op jit(solution)/shard_map/ppermute | solution.py:278
  125.1 2.8 %collective-permute-start.19 = (f32[4,120,28]{2,1,0:T(8,128)S(1)}, f32[4,120,28]{2,1,0:T(8,128)S(1)}, u32[]{:S(2)}, u32[]{:S(2)}) collective-permute-start(f32[4,120,28]{2,1,0:T(8,128)S(1)} %get-tuple-element.98), channel_id=1, source_target_pairs={{0,1},{1,0},{2,3},{3,2},{4,5},{5,4},{6,7},{7,6},{8,9},{9,8},{10,11... | collective-permute-start | bytes 161288 | tf_op jit(solution)/shard_map/ppermute | solution.py:278
  127.9 2.7 %collective-permute-done.15 = f32[4,120,28]{2,1,0:T(8,128)S(1)} collective-permute-done((f32[4,120,28]{2,1,0:T(8,128)S(1)}, f32[4,120,28]{2,1,0:T(8,128)S(1)}, u32[]{:S(2)}, u32[]{:S(2)}) %collective-permute-start.15) | collective-permute-done | bytes 53792 | tf_op jit(solution)/shard_map/ppermute | solution.py:278
  131.1 8.8 %shard_map.66 = (f32[4,64,256]{2,1,0:T(8,128)S(1)}, f32[4,64,256]{2,1,0:T(8,128)S(1)}) custom-call(f32[4,120,312]{2,1,0:T(8,128)S(1)} %pad_maximum_fusion.2.tile_ref, f32[4,106,298]{2,1,0:T(8,128)S(1)} %get-tuple-element.227.t_ref, bf16[128,192]{1,0:T(8,128)(2,1)S(1)} %get-tuple-element.140.a_ref, bf16[4,768,256]{2,1,0:T(8,128)(2,1)S(1)} %get-tuple-element.43.c_ref), custom_call_target="tpu_custom_call" | custom-call | flops 3472883712 | bytes 599040 | tf_op jit(solution)/shard_map/pallas_call | solution.py:224
  140.6 4.2 %collective-permute-start.22 = (f32[4,28,256]{2,1,0:T(8,128)S(1)}, f32[4,28,256]{2,1,0:T(8,128)S(1)}, u32[]{:S(2)}, u32[]{:S(2)}) collective-permute-start(f32[4,28,256]{2,1,0:T(8,128)S(1)} %get-tuple-element.128), channel_id=1, source_target_pairs={{0,2},{1,3},{2,0},{3,1},{4,6},{5,7},{6,4},{7,5},{8,10},{9,11},{10,... | collective-permute-start | bytes 344072 | tf_op jit(solution)/shard_map/ppermute | solution.py:278
  145.2 8.8 %shard_map.67 = (f32[4,64,256]{2,1,0:T(8,128)S(1)}, f32[4,64,256]{2,1,0:T(8,128)S(1)}) custom-call(f32[4,120,312]{2,1,0:T(8,128)S(1)} %pad_maximum_fusion.3.tile_ref, f32[4,106,298]{2,1,0:T(8,128)S(1)} %get-tuple-element.227.t_ref, bf16[128,192]{1,0:T(8,128)(2,1)S(1)} %get-tuple-element.139.a_ref, bf16[4,768,256]{2,1,0:T(8,128)(2,1)S(1)} %get-tuple-element.42.c_ref), custom_call_target="tpu_custom_call" | custom-call | flops 3472883712 | bytes 599040 | tf_op jit(solution)/shard_map/pallas_call | solution.py:224
  158.7 5.4 %collective-permute-start.24 = (f32[4,120,28]{2,1,0:T(8,128)S(1)}, f32[4,120,28]{2,1,0:T(8,128)S(1)}, u32[]{:S(2)}, u32[]{:S(2)}) collective-permute-start(f32[4,120,28]{2,1,0:T(8,128)S(1)} %get-tuple-element.94), channel_id=1, source_target_pairs={{0,1},{1,0},{2,3},{3,2},{4,5},{5,4},{6,7},{7,6},{8,9},{9,8},{10,11... | collective-permute-start | bytes 161288 | tf_op jit(solution)/shard_map/ppermute | solution.py:278
  166.3 4.5 %collective-permute-done.24 = f32[4,120,28]{2,1,0:T(8,128)S(1)} collective-permute-done((f32[4,120,28]{2,1,0:T(8,128)S(1)}, f32[4,120,28]{2,1,0:T(8,128)S(1)}, u32[]{:S(2)}, u32[]{:S(2)}) %collective-permute-start.24) | collective-permute-done | bytes 53792 | tf_op jit(solution)/shard_map/ppermute | solution.py:278
  171.2 8.8 %shard_map.68 = (f32[4,64,256]{2,1,0:T(8,128)S(1)}, f32[4,64,256]{2,1,0:T(8,128)S(1)}) custom-call(f32[4,120,312]{2,1,0:T(8,128)S(1)} %pad_maximum_fusion.4.tile_ref, f32[4,106,298]{2,1,0:T(8,128)S(1)} %get-tuple-element.246.t_ref, bf16[128,192]{1,0:T(8,128)(2,1)S(1)} %get-tuple-element.140.a_ref, bf16[4,768,256]{2,1,0:T(8,128)(2,1)S(1)} %get-tuple-element.43.c_ref), custom_call_target="tpu_custom_call" | custom-call | flops 3472883712 | bytes 599040 | tf_op jit(solution)/shard_map/pallas_call | solution.py:224
  180.8 2.7 %collective-permute-start.33 = (f32[4,28,256]{2,1,0:T(8,128)S(1)}, f32[4,28,256]{2,1,0:T(8,128)S(1)}, u32[]{:S(2)}, u32[]{:S(2)}) collective-permute-start(f32[4,28,256]{2,1,0:T(8,128)S(1)} %get-tuple-element.124), channel_id=1, source_target_pairs={{0,2},{1,3},{2,0},{3,1},{4,6},{5,7},{6,4},{7,5},{8,10},{9,11},{10,... | collective-permute-start | bytes 344072 | tf_op jit(solution)/shard_map/ppermute | solution.py:278
  183.8 8.8 %shard_map.69 = (f32[4,64,256]{2,1,0:T(8,128)S(1)}, f32[4,64,256]{2,1,0:T(8,128)S(1)}) custom-call(f32[4,120,312]{2,1,0:T(8,128)S(1)} %pad_maximum_fusion.5.tile_ref, f32[4,106,298]{2,1,0:T(8,128)S(1)} %get-tuple-element.246.t_ref, bf16[128,192]{1,0:T(8,128)(2,1)S(1)} %get-tuple-element.139.a_ref, bf16[4,768,256]{2,1,0:T(8,128)(2,1)S(1)} %get-tuple-element.42.c_ref), custom_call_target="tpu_custom_call" | custom-call | flops 3472883712 | bytes 599040 | tf_op jit(solution)/shard_map/pallas_call | solution.py:224
  196.3 3.4 %collective-permute-start.35 = (f32[4,120,28]{2,1,0:T(8,128)S(1)}, f32[4,120,28]{2,1,0:T(8,128)S(1)}, u32[]{:S(2)}, u32[]{:S(2)}) collective-permute-start(f32[4,120,28]{2,1,0:T(8,128)S(1)} %get-tuple-element.90), channel_id=1, source_target_pairs={{0,1},{1,0},{2,3},{3,2},{4,5},{5,4},{6,7},{7,6},{8,9},{9,8},{10,11... | collective-permute-start | bytes 161288 | tf_op jit(solution)/shard_map/ppermute | solution.py:278
  200.6 3.3 %collective-permute-start.39 = (f32[4,120,28]{2,1,0:T(8,128)S(1)}, f32[4,120,28]{2,1,0:T(8,128)S(1)}, u32[]{:S(2)}, u32[]{:S(2)}) collective-permute-start(f32[4,120,28]{2,1,0:T(8,128)S(1)} %get-tuple-element.82), channel_id=1, source_target_pairs={{0,1},{1,0},{2,3},{3,2},{4,5},{5,4},{6,7},{7,6},{8,9},{9,8},{10,11... | collective-permute-start | bytes 161288 | tf_op jit(solution)/shard_map/ppermute | solution.py:278
  206.3 9.4 %shard_map.70 = (f32[4,64,256]{2,1,0:T(8,128)}, f32[4,64,256]{2,1,0:T(8,128)S(1)}) custom-call(f32[4,120,312]{2,1,0:T(8,128)S(1)} %pad_maximum_fusion.6.tile_ref, f32[4,106,298]{2,1,0:T(8,128)S(1)} %get-tuple-element.245.t_ref, bf16[128,192]{1,0:T(8,128)(2,1)S(1)} %get-tuple-element.140.a_ref, bf16[4,768,256]{2,1,0:T(8,128)(2,1)S(1)} %get-tuple-element.43.c_ref), custom_call_target="tpu_custom_call" | custom-call | flops 3472883712 | bytes 599040 | tf_op jit(solution)/shard_map/pallas_call | solution.py:224
  216.1 9.4 %shard_map.71 = (f32[4,64,256]{2,1,0:T(8,128)}, f32[4,64,256]{2,1,0:T(8,128)S(1)}) custom-call(f32[4,120,312]{2,1,0:T(8,128)S(1)} %pad_maximum_fusion.7.tile_ref, f32[4,106,298]{2,1,0:T(8,128)S(1)} %get-tuple-element.245.t_ref, bf16[128,192]{1,0:T(8,128)(2,1)S(1)} %get-tuple-element.139.a_ref, bf16[4,768,256]{2,1,0:T(8,128)(2,1)S(1)} %get-tuple-element.42.c_ref), custom_call_target="tpu_custom_call" | custom-call | flops 3472883712 | bytes 599040 | tf_op jit(solution)/shard_map/pallas_call | solution.py:224
  233.4 3.9 %collective-permute-done.42 = f32[4,32,256]{2,1,0:T(8,128)S(1)} collective-permute-done((f32[4,32,256]{2,1,0:T(8,128)S(1)}, f32[4,32,256]{2,1,0:T(8,128)S(1)}, u32[]{:S(2)}, u32[]{:S(2)}) %collective-permute-start.42) | collective-permute-done | bytes 131104 | tf_op jit(solution)/shard_map/ppermute | solution.py:278
  (247 shorter events, 76.9 us)
Async XLA Ops:
  3.7 39.8 %collective-permute-start.3 = (s32[2,4,32,298]{3,2,1,0:T(8,128)}, s32[2,4,32,298]{3,2,1,0:T(8,128)}, u32[]{:S(2)}, u32[]{:S(2)}) collective-permute-start(s32[2,4,32,298]{3,2,1,0:T(8,128)} %get-tuple-element.56), channel_id=1, source_target_pairs={{0,16},{1,17},{2,18},{3,19},{4,20},{5,21},{6,22},{7,23},{8,24},{9,... | collective-permute-start | bytes 915464 | tf_op jit(solution)/shard_map/ppermute | solution.py:278
  6.6 38.2 %collective-permute-start.4 = (s32[2,4,32,298]{3,2,1,0:T(8,128)}, s32[2,4,32,298]{3,2,1,0:T(8,128)}, u32[]{:S(2)}, u32[]{:S(2)}) collective-permute-start(s32[2,4,32,298]{3,2,1,0:T(8,128)} %get-tuple-element.57), channel_id=1, source_target_pairs={{0,1},{1,0},{2,3},{3,2},{4,5},{5,4},{6,7},{7,6},{8,9},{9,8},{10,11... | collective-permute-start | bytes 915464 | tf_op jit(solution)/shard_map/ppermute | solution.py:278
  8.1 36.7 %collective-permute-start.5 = (s32[2,4,32,298]{3,2,1,0:T(8,128)}, s32[2,4,32,298]{3,2,1,0:T(8,128)}, u32[]{:S(2)}, u32[]{:S(2)}) collective-permute-start(s32[2,4,32,298]{3,2,1,0:T(8,128)} %get-tuple-element.58), channel_id=1, source_target_pairs={{0,17},{1,16},{2,19},{3,18},{4,21},{5,20},{6,23},{7,22},{8,25},{9,... | collective-permute-start | bytes 915464 | tf_op jit(solution)/shard_map/ppermute | solution.py:278
  10.5 27.2 %collective-permute-start = (f32[4,32,312]{2,1,0:T(8,128)}, f32[4,32,312]{2,1,0:T(8,128)}, u32[]{:S(2)}, u32[]{:S(2)}) collective-permute-start(f32[4,32,312]{2,1,0:T(8,128)} %dynamic-slice_bitcast_fusion.1), channel_id=1, source_target_pairs={{0,1},{1,0},{2,3},{3,2},{4,5},{5,4},{6,7},{7,6},{8,9},{9,8},{10,11... | collective-permute-start | bytes 479240 | tf_op jit(solution)/shard_map/ppermute | solution.py:278
  13.3 21.0 %collective-permute-start.9 = (f32[4,32,312]{2,1,0:T(8,128)}, f32[4,32,312]{2,1,0:T(8,128)}, u32[]{:S(2)}, u32[]{:S(2)}) collective-permute-start(f32[4,32,312]{2,1,0:T(8,128)} %dynamic-slice_bitcast_fusion), channel_id=1, source_target_pairs={{0,1},{1,0},{2,3},{3,2},{4,5},{5,4},{6,7},{7,6},{8,9},{9,8},{10,11... | collective-permute-start | bytes 479240 | tf_op jit(solution)/shard_map/ppermute | solution.py:278
  36.3 36.3 %collective-permute-start.10 = (f32[4,28,312]{2,1,0:T(8,128)}, f32[4,28,312]{2,1,0:T(8,128)}, u32[]{:S(2)}, u32[]{:S(2)}) collective-permute-start(f32[4,28,312]{2,1,0:T(8,128)} %get-tuple-element.105), channel_id=1, source_target_pairs={{2,4},{3,5},{4,2},{5,3},{10,12},{11,13},{12,10},{13,11},{18,20},{1... | collective-permute-start | bytes 419336 | tf_op jit(solution)/shard_map/ppermute | solution.py:278
  37.7 35.5 %collective-permute-start.11 = (f32[4,28,312]{2,1,0:T(8,128)}, f32[4,28,312]{2,1,0:T(8,128)}, u32[]{:S(2)}, u32[]{:S(2)}) collective-permute-start(f32[4,28,312]{2,1,0:T(8,128)} %get-tuple-element.106), channel_id=1, source_target_pairs={{0,2},{1,3},{2,0},{3,1},{4,6},{5,7},{6,4},{7,5},{8,10},{9,11},{10,... | collective-permute-start | bytes 419336 | tf_op jit(solution)/shard_map/ppermute | solution.py:278
  43.5 32.7 %collective-permute-start.1 = (f32[4,28,312]{2,1,0:T(8,128)}, f32[4,28,312]{2,1,0:T(8,128)}, u32[]{:S(2)}, u32[]{:S(2)}) collective-permute-start(f32[4,28,312]{2,1,0:T(8,128)} %get-tuple-element.109), channel_id=1, source_target_pairs={{2,4},{3,5},{4,2},{5,3},{10,12},{11,13},{12,10},{13,11},{18,20},{1... | collective-permute-start | bytes 419336 | tf_op jit(solution)/shard_map/ppermute | solution.py:278
  47.4 8.9 %collective-permute-start.7 = (s32[2,4,21,298]{3,2,1,0:T(8,128)S(1)}, s32[2,4,21,298]{3,2,1,0:T(8,128)S(1)}, u32[]{:S(2)}, u32[]{:S(2)}) collective-permute-start(s32[2,4,21,298]{3,2,1,0:T(8,128)S(1)} %get-tuple-element.68), channel_id=1, source_target_pairs={{0,2},{1,3},{2,0},{3,1},{4,6},{5,7},{6,4},{7,5},{8,10},{9,11},{10,... | collective-permute-start | bytes 600776 | tf_op jit(solution)/shard_map/ppermute | solution.py:278
  52.2 13.2 %collective-permute-start.25 = (s32[2,4,21,298]{3,2,1,0:T(8,128)}, s32[2,4,21,298]{3,2,1,0:T(8,128)}, u32[]{:S(2)}, u32[]{:S(2)}) collective-permute-start(s32[2,4,21,298]{3,2,1,0:T(8,128)} %get-tuple-element.63), channel_id=1, source_target_pairs={{2,4},{3,5},{4,2},{5,3},{10,12},{11,13},{12,10},{13,11},{18,20},{1... | collective-permute-start | bytes 600776 | tf_op jit(solution)/shard_map/ppermute | solution.py:278
  56.3 10.7 %collective-permute-start.26 = (s32[2,4,21,298]{3,2,1,0:T(8,128)}, s32[2,4,21,298]{3,2,1,0:T(8,128)}, u32[]{:S(2)}, u32[]{:S(2)}) collective-permute-start(s32[2,4,21,298]{3,2,1,0:T(8,128)} %get-tuple-element.64), channel_id=1, source_target_pairs={{0,2},{1,3},{2,0},{3,1},{4,6},{5,7},{6,4},{7,5},{8,10},{9,11},{10,... | collective-permute-start | bytes 600776 | tf_op jit(solution)/shard_map/ppermute | solution.py:278
  65.4 10.8 %collective-permute-start.2 = (f32[4,28,312]{2,1,0:T(8,128)}, f32[4,28,312]{2,1,0:T(8,128)}, u32[]{:S(2)}, u32[]{:S(2)}) collective-permute-start(f32[4,28,312]{2,1,0:T(8,128)} %get-tuple-element.110), channel_id=1, source_target_pairs={{0,2},{1,3},{2,0},{3,1},{4,6},{5,7},{6,4},{7,5},{8,10},{9,11},{10,... | collective-permute-start | bytes 419336 | tf_op jit(solution)/shard_map/ppermute | solution.py:278
  67.0 11.2 %collective-permute-start.8 = (s32[2,4,106,298]{2,1,3,0:T(4,128)}, s32[2,4,106,298]{2,1,3,0:T(4,128)}, u32[]{:S(2)}, u32[]{:S(2)}) collective-permute-start(s32[2,4,106,298]{2,1,3,0:T(4,128)} %copy.8), channel_id=1, source_target_pairs={{0,8},{1,9},{2,10},{3,11},{4,12},{5,13},{6,14},{7,15},{8,0},{9,1},... | collective-permute-start | bytes 3032456 | tf_op jit(solution)/shard_map/ppermute | solution.py:278
  72.6 11.6 %collective-permute-start.27 = (s32[2,4,106,298]{2,1,3,0:T(4,128)}, s32[2,4,106,298]{2,1,3,0:T(4,128)}, u32[]{:S(2)}, u32[]{:S(2)}) collective-permute-start(s32[2,4,106,298]{2,1,3,0:T(4,128)} %copy.12), channel_id=1, source_target_pairs={{0,8},{1,9},{2,10},{3,11},{4,12},{5,13},{6,14},{7,15},{8,0},{9,1},... | collective-permute-start | bytes 3032456 | tf_op jit(solution)/shard_map/ppermute | solution.py:278
  99.4 24.8 %collective-permute-start.16 = (f32[4,28,256]{2,1,0:T(8,128)S(1)}, f32[4,28,256]{2,1,0:T(8,128)S(1)}, u32[]{:S(2)}, u32[]{:S(2)}) collective-permute-start(f32[4,28,256]{2,1,0:T(8,128)S(1)} %get-tuple-element.131), channel_id=1, source_target_pairs={{2,4},{3,5},{4,2},{5,3},{10,12},{11,13},{12,10},{13,11},{18,20},{1... | collective-permute-start | bytes 344072 | tf_op jit(solution)/shard_map/ppermute | solution.py:278
  100.0 24.1 %collective-permute-start.17 = (f32[4,28,256]{2,1,0:T(8,128)S(1)}, f32[4,28,256]{2,1,0:T(8,128)S(1)}, u32[]{:S(2)}, u32[]{:S(2)}) collective-permute-start(f32[4,28,256]{2,1,0:T(8,128)S(1)} %get-tuple-element.132), channel_id=1, source_target_pairs={{0,2},{1,3},{2,0},{3,1},{4,6},{5,7},{6,4},{7,5},{8,10},{9,11},{10,... | collective-permute-start | bytes 344072 | tf_op jit(solution)/shard_map/ppermute | solution.py:278
  120.8 9.8 %collective-permute-start.15 = (f32[4,120,28]{2,1,0:T(8,128)S(1)}, f32[4,120,28]{2,1,0:T(8,128)S(1)}, u32[]{:S(2)}, u32[]{:S(2)}) collective-permute-start(f32[4,120,28]{2,1,0:T(8,128)S(1)} %get-tuple-element.102), channel_id=1, source_target_pairs={{0,1},{1,0},{2,3},{3,2},{4,5},{5,4},{6,7},{7,6},{8,9},{9,8},{10,11... | collective-permute-start | bytes 161288 | tf_op jit(solution)/shard_map/ppermute | solution.py:278
  124.4 20.4 %collective-permute-start.18 = (f32[4,120,28]{2,1,0:T(8,128)S(1)}, f32[4,120,28]{2,1,0:T(8,128)S(1)}, u32[]{:S(2)}, u32[]{:S(2)}) collective-permute-start(f32[4,120,28]{2,1,0:T(8,128)S(1)} %get-tuple-element.97), channel_id=1, source_target_pairs={{1,17},{3,19},{5,21},{7,23},{9,25},{11,27},{13,29},{15,31},{17,1},... | collective-permute-start | bytes 161288 | tf_op jit(solution)/shard_map/ppermute | solution.py:278
  125.1 19.7 %collective-permute-start.19 = (f32[4,120,28]{2,1,0:T(8,128)S(1)}, f32[4,120,28]{2,1,0:T(8,128)S(1)}, u32[]{:S(2)}, u32[]{:S(2)}) collective-permute-start(f32[4,120,28]{2,1,0:T(8,128)S(1)} %get-tuple-element.98), channel_id=1, source_target_pairs={{0,1},{1,0},{2,3},{3,2},{4,5},{5,4},{6,7},{7,6},{8,9},{9,8},{10,11... | collective-permute-start | bytes 161288 | tf_op jit(solution)/shard_map/ppermute | solution.py:278
  139.9 17.9 %collective-permute-start.21 = (f32[4,28,256]{2,1,0:T(8,128)S(1)}, f32[4,28,256]{2,1,0:T(8,128)S(1)}, u32[]{:S(2)}, u32[]{:S(2)}) collective-permute-start(f32[4,28,256]{2,1,0:T(8,128)S(1)} %get-tuple-element.127), channel_id=1, source_target_pairs={{2,4},{3,5},{4,2},{5,3},{10,12},{11,13},{12,10},{13,11},{18,20},{1... | collective-permute-start | bytes 344072 | tf_op jit(solution)/shard_map/ppermute | solution.py:278
  140.6 17.2 %collective-permute-start.22 = (f32[4,28,256]{2,1,0:T(8,128)S(1)}, f32[4,28,256]{2,1,0:T(8,128)S(1)}, u32[]{:S(2)}, u32[]{:S(2)}) collective-permute-start(f32[4,28,256]{2,1,0:T(8,128)S(1)} %get-tuple-element.128), channel_id=1, source_target_pairs={{0,2},{1,3},{2,0},{3,1},{4,6},{5,7},{6,4},{7,5},{8,10},{9,11},{10,... | collective-permute-start | bytes 344072 | tf_op jit(solution)/shard_map/ppermute | solution.py:278
  154.1 10.0 %collective-permute-start.28 = (f32[4,28,256]{2,1,0:T(8,128)S(1)}, f32[4,28,256]{2,1,0:T(8,128)S(1)}, u32[]{:S(2)}, u32[]{:S(2)}) collective-permute-start(f32[4,28,256]{2,1,0:T(8,128)S(1)} %get-tuple-element.119), channel_id=1, source_target_pairs={{2,4},{3,5},{4,2},{5,3},{10,12},{11,13},{12,10},{13,11},{18,20},{1... | collective-permute-start | bytes 344072 | tf_op jit(solution)/shard_map/ppermute | solution.py:278
  155.0 9.1 %collective-permute-start.29 = (f32[4,28,256]{2,1,0:T(8,128)S(1)}, f32[4,28,256]{2,1,0:T(8,128)S(1)}, u32[]{:S(2)}, u32[]{:S(2)}) collective-permute-start(f32[4,28,256]{2,1,0:T(8,128)S(1)} %get-tuple-element.120), channel_id=1, source_target_pairs={{0,2},{1,3},{2,0},{3,1},{4,6},{5,7},{6,4},{7,5},{8,10},{9,11},{10,... | collective-permute-start | bytes 344072 | tf_op jit(solution)/shard_map/ppermute | solution.py:278
  157.8 68.4 %collective-permute-start.20 = (f32[4,64,256]{2,1,0:T(8,128)}, f32[4,64,256]{2,1,0:T(8,128)}, u32[]{:S(2)}, u32[]{:S(2)}) collective-permute-start(f32[4,64,256]{2,1,0:T(8,128)} %broadcast_select_fusion.15), channel_id=1, source_target_pairs={{0,8},{1,9},{2,10},{3,11},{4,12},{5,13},{6,14},{7,15},{8,0},{9,1},... | collective-permute-start | bytes 786440 | tf_op jit(solution)/shard_map/ppermute | solution.py:278
  158.7 12.1 %collective-permute-start.24 = (f32[4,120,28]{2,1,0:T(8,128)S(1)}, f32[4,120,28]{2,1,0:T(8,128)S(1)}, u32[]{:S(2)}, u32[]{:S(2)}) collective-permute-start(f32[4,120,28]{2,1,0:T(8,128)S(1)} %get-tuple-element.94), channel_id=1, source_target_pairs={{0,1},{1,0},{2,3},{3,2},{4,5},{5,4},{6,7},{7,6},{8,9},{9,8},{10,11... | collective-permute-start | bytes 161288 | tf_op jit(solution)/shard_map/ppermute | solution.py:278
  164.3 19.1 %collective-permute-start.30 = (f32[4,120,28]{2,1,0:T(8,128)S(1)}, f32[4,120,28]{2,1,0:T(8,128)S(1)}, u32[]{:S(2)}, u32[]{:S(2)}) collective-permute-start(f32[4,120,28]{2,1,0:T(8,128)S(1)} %get-tuple-element.85), channel_id=1, source_target_pairs={{1,17},{3,19},{5,21},{7,23},{9,25},{11,27},{13,29},{15,31},{17,1},... | collective-permute-start | bytes 161288 | tf_op jit(solution)/shard_map/ppermute | solution.py:278
  165.0 18.4 %collective-permute-start.31 = (f32[4,120,28]{2,1,0:T(8,128)S(1)}, f32[4,120,28]{2,1,0:T(8,128)S(1)}, u32[]{:S(2)}, u32[]{:S(2)}) collective-permute-start(f32[4,120,28]{2,1,0:T(8,128)S(1)} %get-tuple-element.86), channel_id=1, source_target_pairs={{0,1},{1,0},{2,3},{3,2},{4,5},{5,4},{6,7},{7,6},{8,9},{9,8},{10,11... | collective-permute-start | bytes 161288 | tf_op jit(solution)/shard_map/ppermute | solution.py:278
  180.1 15.3 %collective-permute-start.32 = (f32[4,28,256]{2,1,0:T(8,128)S(1)}, f32[4,28,256]{2,1,0:T(8,128)S(1)}, u32[]{:S(2)}, u32[]{:S(2)}) collective-permute-start(f32[4,28,256]{2,1,0:T(8,128)S(1)} %get-tuple-element.123), channel_id=1, source_target_pairs={{2,4},{3,5},{4,2},{5,3},{10,12},{11,13},{12,10},{13,11},{18,20},{1... | collective-permute-start | bytes 344072 | tf_op jit(solution)/shard_map/ppermute | solution.py:278
  180.8 14.7 %collective-permute-start.33 = (f32[4,28,256]{2,1,0:T(8,128)S(1)}, f32[4,28,256]{2,1,0:T(8,128)S(1)}, u32[]{:S(2)}, u32[]{:S(2)}) collective-permute-start(f32[4,28,256]{2,1,0:T(8,128)S(1)} %get-tuple-element.124), channel_id=1, source_target_pairs={{0,2},{1,3},{2,0},{3,1},{4,6},{5,7},{6,4},{7,5},{8,10},{9,11},{10,... | collective-permute-start | bytes 344072 | tf_op jit(solution)/shard_map/ppermute | solution.py:278
  196.3 9.6 %collective-permute-start.35 = (f32[4,120,28]{2,1,0:T(8,128)S(1)}, f32[4,120,28]{2,1,0:T(8,128)S(1)}, u32[]{:S(2)}, u32[]{:S(2)}) collective-permute-start(f32[4,120,28]{2,1,0:T(8,128)S(1)} %get-tuple-element.90), channel_id=1, source_target_pairs={{0,1},{1,0},{2,3},{3,2},{4,5},{5,4},{6,7},{7,6},{8,9},{9,8},{10,11... | collective-permute-start | bytes 161288 | tf_op jit(solution)/shard_map/ppermute | solution.py:278
  199.9 15.8 %collective-permute-start.38 = (f32[4,120,28]{2,1,0:T(8,128)S(1)}, f32[4,120,28]{2,1,0:T(8,128)S(1)}, u32[]{:S(2)}, u32[]{:S(2)}) collective-permute-start(f32[4,120,28]{2,1,0:T(8,128)S(1)} %get-tuple-element.81), channel_id=1, source_target_pairs={{1,17},{3,19},{5,21},{7,23},{9,25},{11,27},{13,29},{15,31},{17,1},... | collective-permute-start | bytes 161288 | tf_op jit(solution)/shard_map/ppermute | solution.py:278
  200.6 15.1 %collective-permute-start.39 = (f32[4,120,28]{2,1,0:T(8,128)S(1)}, f32[4,120,28]{2,1,0:T(8,128)S(1)}, u32[]{:S(2)}, u32[]{:S(2)}) collective-permute-start(f32[4,120,28]{2,1,0:T(8,128)S(1)} %get-tuple-element.82), channel_id=1, source_target_pairs={{0,1},{1,0},{2,3},{3,2},{4,5},{5,4},{6,7},{7,6},{8,9},{9,8},{10,11... | collective-permute-start | bytes 161288 | tf_op jit(solution)/shard_map/ppermute | solution.py:278
  (50 other events, 382.6 us)

commit v2 on v1

--- a/solution.py
+++ b/solution.py
@@ -101,23 +101,193 @@
     return jnp.concatenate(pieces, axis=1)
 
 
+CORE, HI, SIDE, EVEN_PAIR, FIRST_PAIR, LAST_PAIR, BLOCK, REL = range(8)
+
+
+def pack_kernel(halo, edge, info, src, rcv, zone, blend, keep, give, mine, send):
+    per_core = mine.shape[0]
+    strip, width = zone.shape[1:]
+    cols = width // 4
+    half = zone.shape[0] // 2
+    core = info[CORE]
+
+    def sides(x, k, n):
+        left = x[:, cols * k - n : cols * k] if k > 0 else jnp.zeros((strip, n), x.dtype)
+        right = x[:, cols * (k + 1) : cols * (k + 1) + n] if k < 3 else jnp.zeros((strip, n), x.dtype)
+        return left, right
+
+    for k in range(4):
+        slot = info[REL + k]
+        for h in range(2):
+            for v in range(half):
+                z = zone[h * half + v] + OFF
+                w = blend[h * half + v]
+                zl, zr = sides(z, k, edge)
+                wl, wr = sides(w, k, edge)
+                rest = jnp.zeros((strip, LANES - 4 * edge), jnp.int32)
+                lanes = jnp.concatenate([zl, zr, wl, wr, rest], axis=1)
+
+                def put(ref):
+                    ref[slot, v, :, 0:cols] = z[:, cols * k : cols * (k + 1)]
+                    ref[slot, v, :, cols : 2 * cols] = w[:, cols * k : cols * (k + 1)]
+                    ref[slot, v, :, 2 * cols : 2 * cols + LANES] = lanes
+
+                pl.when(core == h)(functools.partial(put, keep))
+                pl.when(core != h)(functools.partial(put, give))
+        for place, ref in ((0, mine), (2, send)):
+
+            @pl.when(slot == place)
+            def _():
+                for q in range(per_core):
+                    at = core * per_core + q
+                    lefts, rights = [], []
+                    for p in range(4):
+                        x = (src if p < 2 else rcv)[p % 2, at]
+                        if p == 3:
+                            x = -x
+                        ref[q, :, p * cols : (p + 1) * cols] = x[:, cols * k : cols * (k + 1)]
+                        left, right = sides(x, k, halo)
+                        lefts.append(left)
+                        rights.append(right)
+                    rest = jnp.zeros((strip, LANES - 4 * halo), f32)
+                    ref[q, :, 4 * cols : 4 * cols + LANES] = jnp.concatenate(lefts + [rest], axis=1)
+                    ref[q, :, 4 * cols + LANES : 4 * cols + 2 * LANES] = jnp.concatenate(
+                        rights + [rest], axis=1
+                    )
+
+
+def edges_out(info, ref, send_a, send_b, count):
+    size = ref.shape[-2]
+    lead = (slice(None),) * (len(ref.shape) - 2)
+
+    def put(top_to, bottom_to):
+        top_to[lead + (slice(0, count),)] = ref[lead + (slice(0, count),)]
+        bottom_to[lead + (slice(0, count),)] = ref[lead + (slice(size - count, size),)]
+
+    pl.when(info[EVEN_PAIR] == 1)(lambda: put(send_b, send_a))
+    pl.when(info[EVEN_PAIR] == 0)(lambda: put(send_a, send_b))
+
+
+def join_tables_kernel(edge, info, mine, got_hi, got_side, got_both, whole, send_a, send_b):
+    strip = mine.shape[1]
+    for s in range(2):
+        near = jnp.where(info[HI] == s, mine[...], got_hi[...])
+        far = jnp.where(info[HI] == s, got_side[...], got_both[...])
+        first = info[SIDE] == 0
+        whole[s, :, 0:strip, :] = jnp.where(first, near, far)
+        whole[s, :, strip : 2 * strip, :] = jnp.where(first, far, near)
+        edges_out(info, whole.at[s], send_a.at[s], send_b.at[s], edge)
+
+
+def join_fields_kernel(halo, info, mine, got, whole, send_a, send_b):
+    strip = mine.shape[0]
+    first = info[SIDE] == 0
+    whole[0:strip, :] = jnp.where(first, mine[...], got[...])
+    whole[strip : 2 * strip, :] = jnp.where(first, got[...], mine[...])
+    edges_out(info, whole, send_a, send_b, halo)
+
+
+def columns_kernel(halo, info, mid, got_a, got_b, send_a, send_b):
+    even = info[EVEN_PAIR] == 1
+    cols = mid.shape[1] // 4
+    lefts, rights = [], []
+    for p in range(4):
+        for start, out in ((p * cols, lefts), ((p + 1) * cols - LANES, rights)):
+            lanes = slice(start, start + LANES)
+            a, b, m = got_a[:, lanes], got_b[:, lanes], mid[:, lanes]
+            top = jnp.where(info[FIRST_PAIR] == 1, 0.0, jnp.where(even, b, a))
+            bottom = jnp.where(info[LAST_PAIR] == 1, 0.0, jnp.where(even, a, b))
+            rows = jnp.concatenate([top, m, bottom], axis=0)
+            out.append(rows[:, :halo] if out is lefts else rows[:, LANES - halo :])
+    rest = jnp.zeros((lefts[0].shape[0], LANES - 4 * halo), f32)
+    left = jnp.concatenate(lefts + [rest], axis=1)
+    right = jnp.concatenate(rights + [rest], axis=1)
+    inner = info[BLOCK] % 2 == 0
+    send_a[...] = jnp.where(inner, right, left)
+    send_b[...] = jnp.where(inner, left, right)
+
+
+def tables_kernel(
+    cols, edge, windows, info, whole_m, whole_o, a_m, a_o, b_m, b_o, out
+):
+    half = whole_m.shape[0]
+    levels, held = out.shape[:2]
+    even = info[EVEN_PAIR] == 1
+    for v in range(levels):
+        own = info[CORE] == v // half
+        i = v % half
+        a = jnp.where(own, a_m[i], a_o[i])[:edge]
+        b = jnp.where(own, b_m[i], b_o[i])[:edge]
+        w = jnp.where(own, whole_m[i], whole_o[i])
+        top = jnp.where(info[FIRST_PAIR] == 1, 0, jnp.where(even, b, a))
+        bottom = jnp.where(info[LAST_PAIR] == 1, 0, jnp.where(even, a, b))
+        x = jnp.concatenate([top, w, bottom], axis=0)
+        s = 2 * cols
+        z = jnp.concatenate([x[:, s : s + edge], x[:, :cols], x[:, s + edge : s + 2 * edge]], 1)
+        s += 2 * edge
+        w = jnp.concatenate(
+            [x[:, s : s + edge], x[:, cols : 2 * cols], x[:, s + edge : s + 2 * edge]], 1
+        )
+        t = (z - OFF).astype(f32) + w.astype(f32) * (1.0 / BLEND)
+        h = x.shape[0] - SPAN * v
+        t = t[HALF * v : HALF * v + h]
+        for b in range(windows):
+            out[v, 0:h, b * LANES : (b + 1) * LANES] = window(t, HALF * v, b)
+        out[v, h:held, :] = jnp.full((held - h, windows * LANES), -8.0, f32)
+
+
 def stage_kernel(
-    levels, rows, cols, windows, blocks, refs,
-    tile_ref, t_ref, a_ref, c_ref, out_ref, img_ref, cur_ref, y_ref, tw_ref, im_ref,
+    levels, halo, windows, blocks, refs, first, last, carried, *args
 ):
-    height = tile_ref.shape[1]
+    args = list(args)
+    info = args.pop(0)
+    mid, got_a, got_b = args[:3]
+    del args[:3]
+    if not first:
+        got_y, got_m = args[:2]
+        del args[:2]
+    tw_ref, a_ref, c_ref = args[:3]
+    del args[:3]
+    if carried:
+        before = args.pop(0)
+    img_ref = args.pop(0)
+    if not last:
+        out_ref, send_a, send_b = args[:3]
+        del args[:3]
+    cur_ref, y_ref, im_ref = args
+    rows = mid.shape[0]
+    cols = img_ref.shape[2]
+    height = rows + 2 * halo
     held = cur_ref.shape[2]
     each = 2 * windows
     lanes = windows * LANES
-    for l in range(levels):
-        h = height - SPAN * (l + 1)
-        x = t_ref[l, HALF * l : HALF * l + h, :]
-        for b in range(windows):
-            tw_ref[l, 0:h, b * LANES : (b + 1) * LANES] = window(x, HALF * l, b)
-        tw_ref[l, h:held, :] = jnp.full((held - h, lanes), -8.0, f32)
+
+    even = info[EVEN_PAIR] == 1
+    inner = info[BLOCK] % 2 == 0
+
+    def rows_of(lane):
+        a, b = got_a[:, lane], got_b[:, lane]
+        top = jnp.where(info[FIRST_PAIR] == 1, 0.0, jnp.where(even, b, a))
+        bottom = jnp.where(info[LAST_PAIR] == 1, 0.0, jnp.where(even, a, b))
+        return jnp.concatenate([top, mid[:, lane], bottom], axis=0)
+
+    if first:
+        left = rows_of(slice(4 * cols, 4 * cols + LANES))
+        right = rows_of(slice(4 * cols + LANES, 4 * cols + 2 * LANES))
+    else:
+        left = jnp.where(info[BLOCK] == 0, 0.0, jnp.where(inner, got_m[...], got_y[...]))
+        right = jnp.where(info[BLOCK] == 3, 0.0, jnp.where(inner, got_y[...], got_m[...]))
     for f in range(2):
         for p in range(2):
-            x = tile_ref[2 * f + p]
+            n = 2 * f + p
+            x = jnp.concatenate(
+                [
+                    left[:, n * halo : (n + 1) * halo],
+                    rows_of(slice(n * cols, (n + 1) * cols)),
+                    right[:, n * halo : (n + 1) * halo],
+                ],
+                axis=1,
+            )
             for b in range(windows):
                 high, low = split(window(x, 0, b))
                 at = (f * windows + b) * LANES
@@ -195,49 +365,41 @@
         return lax.fori_loop(0, count, functools.partial(chunk, l), carry)
 
     lax.fori_loop(0, levels, level, 0)
-    for f in range(2):
-        for p in range(2):
-
-            def get(b):
-                at = (f * windows + b) * LANES
-                return cur_ref[p, 0, 0:rows, at : at + LANES].astype(f32) + cur_ref[
-                    p, 1, 0:rows, at : at + LANES
-                ].astype(f32)
-
-            out_ref[2 * f + p] = dense(get, 0, cols)
+    if not last:
+        for f in range(2):
+            for p in range(2):
+
+                def get(b):
+                    at = (f * windows + b) * LANES
+                    return cur_ref[p, 0, 0:rows, at : at + LANES].astype(f32) + cur_ref[
+                        p, 1, 0:rows, at : at + LANES
+                    ].astype(f32)
+
+                n = 2 * f + p
+                out_ref[:, n * cols : (n + 1) * cols] = dense(get, 0, cols)
+        edges_out(info, out_ref, send_a, send_b, halo)
     for l in range(levels):
         o = HALF * (levels - 1 - l)
-        img_ref[l] = dense(
+        part = dense(
             lambda b: im_ref[l, o : o + rows, b * LANES : (b + 1) * LANES], o, cols
         )
-
-
-def stage(tile, t, by_rows, by_cols, rows, cols, blocks=4):
-    levels = t.shape[0]
-    height = tile.shape[1]
-    refs = by_cols.shape[0]
-    windows = cdiv(cols + SPAN * (levels - 1), WIN)
-    step = BLK * blocks
-    held = max(cdiv(height - SPAN, step) * step + BLK, cdiv(height, BLK) * BLK)
-    body = functools.partial(stage_kernel, levels, rows, cols, windows, blocks, refs)
-    area = levels * (height + rows) // 2 * windows * LANES
+        img_ref[l] = part + before[l] if carried else part
+
+
+def call(body, out_shape, info, *args, **more):
+    specs = [pl.BlockSpec(memory_space=pltpu.SMEM)] + [pl.BlockSpec(memory_space=pltpu.VMEM)] * len(args)
     return pl.pallas_call(
         body,
-        out_shape=[
-            jax.ShapeDtypeStruct((4, rows, cols), f32),
-            jax.ShapeDtypeStruct((levels, rows, cols), f32),
-        ],
-        scratch_shapes=[
-            pltpu.VMEM((2, 2, held, 2 * windows * LANES), bf16),
-            pltpu.VMEM((refs, blocks * 2 * windows * BLK, 4 * LANES), bf16),
-            pltpu.VMEM((levels, held, windows * LANES), f32),
-            pltpu.VMEM((levels, held, windows * LANES), f32),
-        ],
+        in_specs=specs,
+        out_specs=jax.tree.map(lambda _: pl.BlockSpec(memory_space=pltpu.VMEM), out_shape),
+        out_shape=out_shape,
         compiler_params=pltpu.CompilerParams(vmem_limit_bytes=40 * 2**20),
-        cost_estimate=pl.CostEstimate(
-            flops=area * 2 * refs * 2 * 3 * 512, bytes_accessed=4 * tile.size, transcendentals=0
-        ),
-    )(tile, t, by_rows, by_cols)
+        **more,
+    )(info, *args)
+
+
+def shape(*dims, dtype=f32):
+    return jax.ShapeDtypeStruct(dims, dtype)
 
 
 def local(source_field, receiver_field, zone_index, blend_weight, ref_velocity, frequencies):
@@ -245,25 +407,30 @@
     d, l = lax.axis_index("depth"), lax.axis_index("lat")
     hi, core = d // 2, d % 2
     pair, side = l // 2, l % 2
-    if depth != 4 or lat % 2:
+    if depth != 4 or lat % 4:
         raise ValueError("mesh")
     levels, strip, width = zone_index.shape
-    freq_count = source_field.shape[1]
+    freq_count, refs = frequencies.shape[0], ref_velocity.shape[0]
     per_core = freq_count // 2
     rows, cols = 2 * strip, width // 4
     halo = HALF * levels
     edge = halo - HALF
+    half = levels // 2
+    windows = cdiv(cols + SPAN * (levels - 1), WIN)
+    blocks = 4
+    step = BLK * blocks
+    held = cdiv(rows + 2 * halo - SPAN, step) * step + BLK
 
     def permutation(move):
         out = []
         for i in range(depth * lat):
             dd, ll = divmod(i, lat)
-            target = move(dd // 2, dd % 2, ll // 2, ll % 2)
-            if target is None:
-                continue
-            h2, c2, p2, s2 = target
-            if 0 <= p2 < lat // 2:
-                out.append((i, (h2 * 2 + c2) * lat + p2 * 2 + s2))
+            h, c, p, s = dd // 2, dd % 2, ll // 2, ll % 2
+            target = move(h, c, p, s)
+            if target is None or not 0 <= target[2] < lat // 2:
+                target = (h, 1 - c, p, s)
+            h, c, p, s = target
+            out.append((i, (h * 2 + c) * lat + p * 2 + s))
         return out
 
     across_hi = permutation(lambda h, c, p, s: (1 - h, c, p, s))
@@ -281,89 +448,144 @@
         return 2 * h + jnp.where(h == 0, s, 1 - s)
 
     block = place(hi, side)
-
-    def exchange_rows(x, count, axis):
-        size = x.shape[axis]
-        top = lax.slice_in_dim(x, 0, count, axis=axis)
-        bottom = lax.slice_in_dim(x, size - count, size, axis=axis)
-        even = pair % 2 == 0
-        got_a = move(jnp.where(even, bottom, top), pairs_even)
-        got_b = move(jnp.where(even, top, bottom), pairs_odd)
-        return jnp.where(even, got_b, got_a), jnp.where(even, got_a, got_b)
-
-    def exchange_cols(x, count):
-        even = block % 2 == 0
-        left, right = x[..., :count], x[..., -count:]
-        got_a = move(jnp.where(even, right, left), across_side)
-        got_b = move(jnp.where(even, left, right), middle)
-        return jnp.where(even, got_b, got_a), jnp.where(even, got_a, got_b)
-
-    def columns(x, which, size):
-        return lax.dynamic_slice_in_dim(x, which * cols, size, x.ndim - 1)
-
-    def by_side(mine, other, axis):
-        return jnp.concatenate(
-            [jnp.where(side == 0, mine, other), jnp.where(side == 0, other, mine)], axis=axis
-        )
-
-    tables = jnp.stack([zone_index + OFF, blend_weight])
-    tables = jnp.pad(tables, ((0, 0),) * 3 + ((edge, edge),))
-    size = cols + 2 * edge
-    mine = columns(tables, block, size)
-    got_hi = move(columns(tables, place(1 - hi, side), size), across_hi)
-    got_side = move(columns(tables, place(hi, 1 - side), size), across_side)
-    got_both = move(columns(tables, place(1 - hi, 1 - side), size), across_both)
-    stage_t = [None] * 4
-    for s in range(2):
-        whole = by_side(
-            jnp.where(hi == s, mine, got_hi), jnp.where(hi == s, got_side, got_both), 2
-        )
-        above, below = exchange_rows(whole, edge, 2)
-        whole = jnp.concatenate([above, whole, below], axis=2)
-        other = move(whole, across_core)
-        for k in range(2):
-            pick = jnp.where(core == k, whole, other)
-            stage_t[2 * s + k] = (pick[0] - OFF).astype(f32) + pick[1].astype(f32) / BLEND
-
-    surface = jnp.stack(
-        [source_field[0], source_field[1], receiver_field[0], -receiver_field[1]], axis=1
+    rel = []
+    for k in range(4):
+        kh = k // 2
+        ks = k % 2 if kh == 0 else 1 - k % 2
+        rel.append(jnp.where(hi == kh, 0, 1) + jnp.where(side == ks, 0, 2))
+    info = jnp.stack(
+        [
+            core,
+            hi,
+            side,
+            (pair % 2 == 0).astype(jnp.int32),
+            (pair == 0).astype(jnp.int32),
+            (pair == lat // 2 - 1).astype(jnp.int32),
+            block,
+        ]
+        + rel
+    ).astype(jnp.int32)
+
+    lane_t = 2 * cols + LANES
+    lane_f = 4 * cols + 2 * LANES
+    packed = shape(4, half, strip, lane_t, dtype=jnp.int32)
+    keep, give, mine, send = call(
+        functools.partial(pack_kernel, halo, edge),
+        [packed, packed] + [shape(per_core, strip, lane_f)] * 2,
+        info,
+        source_field,
+        receiver_field,
+        zone_index,
+        blend_weight,
     )
-    surface = lax.dynamic_slice_in_dim(surface, core * per_core, per_core, 0)
-    surface = jnp.pad(surface, ((0, 0),) * 3 + ((halo, halo),))
-    size = cols + 2 * halo
-    tiles = []
+    swapped = move(give, across_core)
+    got = [move(send[q], across_side) for q in range(per_core)]
+
+    def spread(k):
+        own = jnp.where(core == k, keep, swapped)
+        return (
+            own[0],
+            move(own[1], across_hi),
+            move(own[2], across_side),
+            move(own[3], across_both),
+        )
+
+    def join(parts):
+        return call(
+            functools.partial(join_tables_kernel, edge),
+            [shape(2, half, rows, lane_t, dtype=jnp.int32)]
+            + [shape(2, half, cdiv(edge, 8) * 8, lane_t, dtype=jnp.int32)] * 2,
+            info,
+            *parts,
+        )
+
+    def finish(whole, send_a, send_b):
+        got_a, got_b = move(send_a, pairs_even), move(send_b, pairs_odd)
+        return call(
+            functools.partial(tables_kernel, cols, edge, windows),
+            shape(levels, held, windows * LANES),
+            info,
+            whole,
+            move(whole, across_core),
+            got_a,
+            move(got_a, across_core),
+            got_b,
+            move(got_b, across_core),
+        )
+
+    tables = [None] * 4
+    joined = [join(spread(0)), None]
+    tables[0] = finish(*[x[0] for x in joined[0]])
+
+    state = []
     for q in range(per_core):
-        mine = columns(surface[q], block, size)
-        other = move(columns(surface[q], place(hi, 1 - side), size), across_side)
-        tile = by_side(mine, other, 1)
-        above, below = exchange_rows(tile, halo, 1)
-        tiles.append(jnp.concatenate([above, tile, below], axis=1))
-
-    tap_re, tap_im, turn_cos, turn_sin = kernels(frequencies, ref_velocity)
-    by_rows, by_cols = operators(tap_re, tap_im, turn_cos, turn_sin)
-    by_rows = lax.dynamic_slice_in_dim(by_rows, core * per_core, per_core, 0)
-    by_cols = lax.dynamic_slice_in_dim(by_cols, core * per_core, per_core, 0)
-
+        whole, send_a, send_b = call(
+            functools.partial(join_fields_kernel, halo),
+            [shape(rows, lane_f), shape(halo, lane_f), shape(halo, lane_f)],
+            info,
+            mine[q],
+            got[q],
+        )
+        state.append((whole, move(send_a, pairs_even), move(send_b, pairs_odd)))
+
+    taps = kernels(frequencies, ref_velocity)
+    taps = [lax.dynamic_slice_in_dim(x, core * per_core, per_core, 0) for x in taps]
+    by_rows, by_cols = operators(*taps)
+
+    area = levels * (rows + halo) * windows * LANES
     images = []
     for s in range(4):
-        image = None
+        image = []
         for q in range(per_core):
-            field, part = stage(tiles[q], stage_t[s], by_rows[q], by_cols[q], rows, cols)
-            image = part if image is None else image + part
+            out_shape = [shape(levels, rows, cols)]
             if s < 3:
-                above, below = exchange_rows(field, halo, 1)
-                field = jnp.concatenate([above, field, below], axis=1)
-                left, right = exchange_cols(field, halo)
-                tiles[q] = jnp.concatenate([left, field, right], axis=2)
+                out_shape += [shape(rows, 4 * cols)] + [shape(halo, 4 * cols)] * 2
+            image, *fields = call(
+                functools.partial(
+                    stage_kernel, levels, halo, windows, blocks, refs, s == 0, s == 3, q > 0
+                ),
+                out_shape,
+                info,
+                *state[q],
+                tables[s],
+                by_rows[q],
+                by_cols[q],
+                *([image] if q else []),
+                scratch_shapes=[
+                    pltpu.VMEM((2, 2, held, 2 * windows * LANES), bf16),
+                    pltpu.VMEM((refs, blocks * 2 * windows * BLK, 4 * LANES), bf16),
+                    pltpu.VMEM((levels, held, windows * LANES), f32),
+                ],
+                cost_estimate=pl.CostEstimate(
+                    flops=area * 2 * refs * 2 * 3 * 512, bytes_accessed=2**21, transcendentals=0
+                ),
+            )
+            if s < 3:
+                field, send_a, send_b = fields
+                got_a, got_b = move(send_a, pairs_even), move(send_b, pairs_odd)
+                side_a, side_b = call(
+                    functools.partial(columns_kernel, halo),
+                    [shape(rows + 2 * halo, LANES)] * 2,
+                    info,
+                    field,
+                    got_a,
+                    got_b,
+                )
+                state[q] = (
+                    field, got_a, got_b, move(side_a, across_side), move(side_b, middle),
+                )
+            if s == 0 and q == 0:
+                keep, swapped, _ = lax.optimization_barrier((keep, swapped, image))
+                joined[1] = join(spread(1))
+                tables[1] = finish(*[x[0] for x in joined[1]])
+                tables[2] = finish(*[x[1] for x in joined[0]])
+                tables[3] = finish(*[x[1] for x in joined[1]])
         images.append(image)
 
-    sums = []
-    for s in range(2):
-        mine = jnp.where(core == 0, images[2 * s], images[2 * s + 1])
-        other = jnp.where(core == 0, images[2 * s + 1], images[2 * s])
-        sums.append(mine + move(other, across_core))
-    here = jnp.where(hi == 0, sums[0], sums[1])
-    there = jnp.where(hi == 0, sums[1], sums[0])
+    sums = [x + move(x, across_core) for x in images]
+    sets = [jnp.where(core == 0, sums[2 * s], sums[2 * s + 1]) for s in range(2)]
+    here = jnp.where(hi == 0, sets[0], sets[1])
+    there = jnp.where(hi == 0, sets[1], sets[0])
 
     def strip_of(x, s):
         return lax.dynamic_slice_in_dim(x, s * strip, strip, 1)

time: 242 us -> 178 us (0.74)
  other arithmetic: 37.1 us -> 5.54 us
  starting transfers between devices: 75.2 us -> 51.5 us
  Pallas kernels: 71.7 us -> 91.2 us
  local copies, waits for them, and re-layouts: 19.3 us -> 5.25 us
  waiting for transfers between devices: 36.2 us -> 23.4 us
    ppermute x44 -> x64, starting transfers between devices: 75.2 us -> 51.5 us  [move(): return lax.ppermute(x, AXES, pairs)]
    pallas_call x8 -> x23, Pallas kernels: 71.7 us -> 91.2 us  [call(): pl.pallas_call(body, in_specs=specs, out_specs=jax.tree.map(lambda _: pl....]
    select_n x41 -> x4, other arithmetic: 19 us -> 0.36 us  [the longest x2 0.18 us: spread(): own = jnp.where(core == k, keep, swapped)]
    ppermute x44 -> x64, waiting for transfers between devices: 36.2 us -> 23.4 us  [move(): return lax.ppermute(x, AXES, pairs)]
    concatenate x16 -> x0, other arithmetic: 7.67 us -> none  [the longest x2 2.85 us: local(): tiles.append(jnp.concatenate([above, tile, below], axis=1))]
    ppermute x2 -> x0, local copies, waits for them, and re-layouts: 5.06 us -> none  [move(): return lax.ppermute(x, AXES, pairs)]
    concatenate x2 -> x0, local copies, waits for them, and re-layouts: 5.01 us -> none  [local(): whole = jnp.concatenate([above, whole, below], axis=2)]
    dynamic_slice x3 -> x2, local copies, waits for them, and re-layouts: 2.98 us -> 0.02 us  [local(): lax.dynamic_slice_in_dim(x, core * per_core, per_core, 0)]
  transfers between devices with their start and end apart: 44 -> 64, of which waited for: 11 -> 12; matrix products, arithmetic and copies ran while one was open for 17% -> 3% of each run, Pallas kernels for 26% -> 50%
where the time goes in v2:
time: 178 us
  Pallas kernels  91.2 us (51%)
  starting transfers between devices  51.5 us (29%)
  waiting for transfers between devices  23.4 us (13%)
  other arithmetic  5.54 us (3%)
  local copies, waits for them, and re-layouts  5.25 us (3%)
    pallas_call x23, Pallas kernels, call(): pl.pallas_call(body, in_specs=specs, out_specs=jax.tree.map(lambda _: pl....  91.2 us
    ppermute x64, starting transfers between devices, move(): return lax.ppermute(x, AXES, pairs)  51.5 us
    ppermute x64, waiting for transfers between devices, move(): return lax.ppermute(x, AXES, pairs)  23.4 us
    unnamed x12, local copies, waits for them, and re-layouts  4.54 us
  transfers between devices with their start and end apart: 64, of which 12 were waited for; matrix products, arithmetic and copies ran while one was open for 3% of the time, Pallas kernels for 50%

profile of v2, /device:TPU:0, one launch (start us, length us, event | category | flops | bytes accessed | tf_op | source)
XLA Modules:
  0.0 177.6 jit_solution(4554924117861151117)
XLA Ops:
  4.6 2.1 %shard_map.64 = (s32[4,2,32,640]{3,2,1,0:T(8,128)S(1)}, s32[4,2,32,640]{3,2,1,0:T(8,128)S(1)}, f32[2,32,1280]{2,1,0:T(8,128)S(1)}, f32[2,32,1280]{2,1,0:T(8,128)S(1)}) custom-call(s32[11]{0:T(128)S(1)} %stack.68.info.args_0_, f32[2,4,32,1024]{3,2,1,0:T(8,128)S(1)} %copy-done, f32[2,4,32,1024]{3,2,1,0:T(8,128)S(1)} %copy-done.1, ...), custom_call_target="tpu_custom_call" | custom-call | tf_op jit(solution)/shard_map/pallas_call | solution.py:391
  6.8 3.0 %collective-permute-start.12 = (f32[32,1280]{1,0:T(8,128)S(1)}, f32[32,1280]{1,0:T(8,128)S(1)}, u32[]{:S(2)}, u32[]{:S(2)}) collective-permute-start(f32[32,1280]{1,0:T(8,128)S(1)} %get-tuple-element.145), channel_id=1, source_target_pairs={{0,1},{1,0},{2,3},{3,2},{4,5},{5,4},{6,7},{7,6},{8,9},{9,8},{10,11... | collective-permute-start | bytes 491528 | tf_op jit(solution)/shard_map/ppermute | solution.py:445
  14.7 1.5 collective-permute-start.6
  16.2 1.5 collective-permute-start.5
  18.2 4.4 %collective-permute-done.6.got_both = s32[2,32,640]{2,1,0:T(8,128)S(1)} collective-permute-done((s32[2,32,640]{2,1,0:T(8,128)S(1)}, s32[2,32,640]{2,1,0:T(8,128)S(1)}, u32[]{:S(2)}, u32[]{:S(2)}) %collective-permute-start.6) | collective-permute-done | bytes 163872 | tf_op jit(solution)/shard_map/ppermute | solution.py:445
  22.7 3.1 %collective-permute-done.5.got_side = s32[2,32,640]{2,1,0:T(8,128)S(1)} collective-permute-done((s32[2,32,640]{2,1,0:T(8,128)S(1)}, s32[2,32,640]{2,1,0:T(8,128)S(1)}, u32[]{:S(2)}, u32[]{:S(2)}) %collective-permute-start.5) | collective-permute-done | bytes 163872 | tf_op jit(solution)/shard_map/ppermute | solution.py:445
  26.5 1.6 collective-permute-start.8
  29.5 2.7 %collective-permute-start.13 = (f32[28,1280]{1,0:T(8,128)S(1)}, f32[28,1280]{1,0:T(8,128)S(1)}, u32[]{:S(2)}, u32[]{:S(2)}) collective-permute-start(f32[28,1280]{1,0:T(8,128)S(1)} %get-tuple-element.70), channel_id=1, source_target_pairs={{0,2},{1,3},{2,0},{3,1},{4,6},{5,7},{6,4},{7,5},{8,10},{9,11},{10,... | collective-permute-start | bytes 430088 | tf_op jit(solution)/shard_map/ppermute | solution.py:445
  37.1 9.6 %shard_map.69 = (f32[4,64,256]{2,1,0:T(8,128)S(1)}, f32[64,1024]{1,0:T(8,128)S(1)}, f32[28,1024]{1,0:T(8,128)S(1)}, f32[28,1024]{1,0:T(8,128)S(1)}) custom-call(s32[11]{0:T(128)S(1)} %stack.68.info.args_0_, f32[64,1280]{1,0:T(8,128)S(1)} %get-tuple-element.69.args_1_, f32[28,1280]{1,0:T(8,128)S(1)} %collective-permute-done.13.args_2_, ...), custom_call_target="tpu_custom_call" | custom-call | flops 3472883712 | bytes 2097152 | tf_op jit(solution)/shard_map/pallas_call | solution.py:391
  46.9 1.6 collective-permute-start.22
  51.0 1.9 %collective-permute-start.1 = (f32[28,1280]{1,0:T(8,128)S(1)}, f32[28,1280]{1,0:T(8,128)S(1)}, u32[]{:S(2)}, u32[]{:S(2)}) collective-permute-start(f32[28,1280]{1,0:T(8,128)S(1)} %get-tuple-element.62), channel_id=1, source_target_pairs={{0,2},{1,3},{2,0},{3,1},{4,6},{5,7},{6,4},{7,5},{8,10},{9,11},{10,... | collective-permute-start | bytes 430088 | tf_op jit(solution)/shard_map/ppermute | solution.py:445
  52.9 2.0 %collective-permute-done.22.got_both = s32[2,32,640]{2,1,0:T(8,128)S(1)} collective-permute-done((s32[2,32,640]{2,1,0:T(8,128)S(1)}, s32[2,32,640]{2,1,0:T(8,128)S(1)}, u32[]{:S(2)}, u32[]{:S(2)}) %collective-permute-start.22) | collective-permute-done | bytes 163872 | tf_op jit(solution)/shard_map/ppermute | solution.py:445
  55.0 1.8 %collective-permute-start.38 = (s32[2,24,640]{2,1,0:T(8,128)S(1)}, s32[2,24,640]{2,1,0:T(8,128)S(1)}, u32[]{:S(2)}, u32[]{:S(2)}) collective-permute-start(s32[2,24,640]{2,1,0:T(8,128)S(1)} %get-tuple-element.157), channel_id=1, source_target_pairs={{0,2},{1,3},{2,0},{3,1},{4,6},{5,7},{6,4},{7,5},{8,10},{9,11},{10,... | collective-permute-start | bytes 368648 | tf_op jit(solution)/shard_map/ppermute | solution.py:445
  57.4 2.7 %collective-permute-start.28 = (f32[28,1024]{1,0:T(8,128)S(1)}, f32[28,1024]{1,0:T(8,128)S(1)}, u32[]{:S(2)}, u32[]{:S(2)}) collective-permute-start(f32[28,1024]{1,0:T(8,128)S(1)} %get-tuple-element.85), channel_id=1, source_target_pairs={{0,2},{1,3},{2,0},{3,1},{4,6},{5,7},{6,4},{7,5},{8,10},{9,11},{10,... | collective-permute-start | bytes 344072 | tf_op jit(solution)/shard_map/ppermute | solution.py:445
  62.6 9.6 %shard_map.70 = (f32[4,64,256]{2,1,0:T(8,128)S(1)}, f32[64,1024]{1,0:T(8,128)S(1)}, f32[28,1024]{1,0:T(8,128)S(1)}, f32[28,1024]{1,0:T(8,128)S(1)}) custom-call(s32[11]{0:T(128)S(1)} %stack.68.info.args_0_, f32[64,1280]{1,0:T(8,128)S(1)} %get-tuple-element.61.args_1_, f32[28,1280]{1,0:T(8,128)S(1)} %collective-permute-done.1.args_2_, ...), custom_call_target="tpu_custom_call" | custom-call | flops 3472883712 | bytes 2097152 | tf_op jit(solution)/shard_map/pallas_call | solution.py:391
  72.2 2.5 %collective-permute-start.16 = (f32[28,1024]{1,0:T(8,128)S(1)}, f32[28,1024]{1,0:T(8,128)S(1)}, u32[]{:S(2)}, u32[]{:S(2)}) collective-permute-start(f32[28,1024]{1,0:T(8,128)S(1)} %get-tuple-element.75), channel_id=1, source_target_pairs={{0,2},{1,3},{2,0},{3,1},{4,6},{5,7},{6,4},{7,5},{8,10},{9,11},{10,... | collective-permute-start | bytes 344072 | tf_op jit(solution)/shard_map/ppermute | solution.py:445
  76.2 2.7 %collective-permute-done.16.got_a.args_2_ = f32[28,1024]{1,0:T(8,128)S(1)} collective-permute-done((f32[28,1024]{1,0:T(8,128)S(1)}, f32[28,1024]{1,0:T(8,128)S(1)}, u32[]{:S(2)}, u32[]{:S(2)}) %collective-permute-start.16) | collective-permute-done | bytes 114720 | tf_op jit(solution)/shard_map/ppermute | solution.py:445
  84.7 9.6 %shard_map.75 = (f32[4,64,256]{2,1,0:T(8,128)S(1)}, f32[64,1024]{1,0:T(8,128)S(1)}, f32[28,1024]{1,0:T(8,128)S(1)}, f32[28,1024]{1,0:T(8,128)S(1)}) custom-call(s32[11]{0:T(128)S(1)} %stack.68.info.args_0_, f32[64,1024]{1,0:T(8,128)S(1)} %get-tuple-element.84.mid.args_1_, f32[28,1024]{1,0:T(8,128)S(1)} %collective-permute-done.28.got_a.args_2_, ...), custom_call_target="tpu_custom_call" | custom-call | flops 3472883712 | bytes 2097152 | tf_op jit(solution)/shard_map/pallas_call | solution.py:391
  94.3 1.8 %collective-permute-start.52 = (s32[2,24,640]{2,1,0:T(8,128)S(1)}, s32[2,24,640]{2,1,0:T(8,128)S(1)}, u32[]{:S(2)}, u32[]{:S(2)}) collective-permute-start(s32[2,24,640]{2,1,0:T(8,128)S(1)} %get-tuple-element.153), channel_id=1, source_target_pairs={{0,2},{1,3},{2,0},{3,1},{4,6},{5,7},{6,4},{7,5},{8,10},{9,11},{10,... | collective-permute-start | bytes 368648 | tf_op jit(solution)/shard_map/ppermute | solution.py:445
  96.9 9.6 %shard_map.76 = (f32[4,64,256]{2,1,0:T(8,128)S(1)}, f32[64,1024]{1,0:T(8,128)S(1)}, f32[28,1024]{1,0:T(8,128)S(1)}, f32[28,1024]{1,0:T(8,128)S(1)}) custom-call(s32[11]{0:T(128)S(1)} %stack.68.info.args_0_, f32[64,1024]{1,0:T(8,128)S(1)} %get-tuple-element.74.mid.args_1_, f32[28,1024]{1,0:T(8,128)S(1)} %collective-permute-done.16.got_a.args_2_, ...), custom_call_target="tpu_custom_call" | custom-call | flops 3472883712 | bytes 2097152 | tf_op jit(solution)/shard_map/pallas_call | solution.py:391
  106.5 1.9 %collective-permute-start.33 = (f32[28,1024]{1,0:T(8,128)S(1)}, f32[28,1024]{1,0:T(8,128)S(1)}, u32[]{:S(2)}, u32[]{:S(2)}) collective-permute-start(f32[28,1024]{1,0:T(8,128)S(1)} %get-tuple-element.92), channel_id=1, source_target_pairs={{0,2},{1,3},{2,0},{3,1},{4,6},{5,7},{6,4},{7,5},{8,10},{9,11},{10,... | collective-permute-start | bytes 344072 | tf_op jit(solution)/shard_map/ppermute | solution.py:445
  109.1 2.1 %collective-permute-start.44 = (f32[120,128]{1,0:T(8,128)S(1)}, f32[120,128]{1,0:T(8,128)S(1)}, u32[]{:S(2)}, u32[]{:S(2)}) collective-permute-start(f32[120,128]{1,0:T(8,128)S(1)} %get-tuple-element.99), channel_id=1, source_target_pairs={{0,1},{1,0},{2,3},{3,2},{4,5},{5,4},{6,7},{7,6},{8,9},{9,8},{10,11... | collective-permute-start | bytes 184328 | tf_op jit(solution)/shard_map/ppermute | solution.py:445
  114.4 1.5 collective-permute-start.35
  116.1 9.8 %shard_map.80 = (f32[4,64,256]{2,1,0:T(8,128)S(1)}, f32[64,1024]{1,0:T(8,128)S(1)}, f32[28,1024]{1,0:T(8,128)S(1)}, f32[28,1024]{1,0:T(8,128)S(1)}) custom-call(s32[11]{0:T(128)S(1)} %stack.68.info.args_0_, f32[64,1024]{1,0:T(8,128)S(1)} %get-tuple-element.96.mid.args_1_, f32[28,1024]{1,0:T(8,128)S(1)} %collective-permute-done.42.got_a.args_2_, ...), custom_call_target="tpu_custom_call" | custom-call | flops 3472883712 | bytes 2097152 | tf_op jit(solution)/shard_map/pallas_call | solution.py:391
  127.2 9.6 %shard_map.81 = (f32[4,64,256]{2,1,0:T(8,128)S(1)}, f32[64,1024]{1,0:T(8,128)S(1)}, f32[28,1024]{1,0:T(8,128)S(1)}, f32[28,1024]{1,0:T(8,128)S(1)}) custom-call(s32[11]{0:T(128)S(1)} %stack.68.info.args_0_, f32[64,1024]{1,0:T(8,128)S(1)} %get-tuple-element.91.mid.args_1_, f32[28,1024]{1,0:T(8,128)S(1)} %collective-permute-done.33.got_a.args_2_, ...), custom_call_target="tpu_custom_call" | custom-call | flops 3472883712 | bytes 2097152 | tf_op jit(solution)/shard_map/pallas_call | solution.py:391
  136.9 1.9 %collective-permute-start.47 = (f32[28,1024]{1,0:T(8,128)S(1)}, f32[28,1024]{1,0:T(8,128)S(1)}, u32[]{:S(2)}, u32[]{:S(2)}) collective-permute-start(f32[28,1024]{1,0:T(8,128)S(1)} %get-tuple-element.104), channel_id=1, source_target_pairs={{0,2},{1,3},{2,0},{3,1},{4,6},{5,7},{6,4},{7,5},{8,10},{9,11},{10,... | collective-permute-start | bytes 344072 | tf_op jit(solution)/shard_map/ppermute | solution.py:445
  139.5 1.5 collective-permute-start.58
  144.2 1.6 collective-permute-start.49
  145.8 9.5 %shard_map.85.args_9_ = f32[4,64,256]{2,1,0:T(8,128)S(1)} custom-call(s32[11]{0:T(128)S(1)} %stack.68.info.args_0_, f32[64,1024]{1,0:T(8,128)S(1)} %get-tuple-element.108.mid.args_1_, f32[28,1024]{1,0:T(8,128)S(1)} %collective-permute-done.56.got_a.args_2_, f32[28,1024]{1,0:T(8,128)S(1)} %collective-permute-done.57.got_b.args_3_, ...), custom_call_target="tpu_custom_call" | custom-call | flops 3472883712 | bytes 2097152 | tf_op jit(solution)/shard_map/pallas_call | solution.py:391
  155.3 9.5 %shard_map.86 = f32[4,64,256]{2,1,0:T(8,128)S(1)} custom-call(s32[11]{0:T(128)S(1)} %stack.68.info.args_0_, f32[64,1024]{1,0:T(8,128)S(1)} %get-tuple-element.103.mid.args_1_, f32[28,1024]{1,0:T(8,128)S(1)} %collective-permute-done.47.got_a.args_2_, f32[28,1024]{1,0:T(8,128)S(1)} %collective-permute-done.48.got_b.args_3_, ...), custom_call_target="tpu_custom_call" | custom-call | flops 3472883712 | bytes 2097152 | tf_op jit(solution)/shard_map/pallas_call | solution.py:391
  166.6 1.6 collective-permute-start.62
  170.4 4.6 %collective-permute-done.62 = f32[4,32,256]{2,1,0:T(8,128)S(1)} collective-permute-done((f32[4,32,256]{2,1,0:T(8,128)S(1)}, f32[4,32,256]{2,1,0:T(8,128)S(1)}, u32[]{:S(2)}, u32[]{:S(2)}) %collective-permute-start.62) | collective-permute-done | bytes 131104 | tf_op jit(solution)/shard_map/ppermute | solution.py:445
  (185 shorter events, 46.3 us)
Async XLA Ops:
  6.8 22.1 %collective-permute-start.12 = (f32[32,1280]{1,0:T(8,128)S(1)}, f32[32,1280]{1,0:T(8,128)S(1)}, u32[]{:S(2)}, u32[]{:S(2)}) collective-permute-start(f32[32,1280]{1,0:T(8,128)S(1)} %get-tuple-element.145), channel_id=1, source_target_pairs={{0,1},{1,0},{2,3},{3,2},{4,5},{5,4},{6,7},{7,6},{8,9},{9,8},{10,11... | collective-permute-start | bytes 491528 | tf_op jit(solution)/shard_map/ppermute | solution.py:445
  16.2 9.6 %collective-permute-start.5 = (s32[2,32,640]{2,1,0:T(8,128)S(1)}, s32[2,32,640]{2,1,0:T(8,128)S(1)}, u32[]{:S(2)}, u32[]{:S(2)}) collective-permute-start(s32[2,32,640]{2,1,0:T(8,128)S(1)} %get-tuple-element.142), channel_id=1, source_target_pairs={{0,1},{1,0},{2,3},{3,2},{4,5},{5,4},{6,7},{7,6},{8,9},{9,8},{10,11... | collective-permute-start | bytes 491528 | tf_op jit(solution)/shard_map/ppermute | solution.py:445
  33.8 16.6 %collective-permute-start = (f32[32,1280]{1,0:T(8,128)S(1)}, f32[32,1280]{1,0:T(8,128)S(1)}, u32[]{:S(2)}, u32[]{:S(2)}) collective-permute-start(f32[32,1280]{1,0:T(8,128)S(1)} %get-tuple-element.146), channel_id=1, source_target_pairs={{0,1},{1,0},{2,3},{3,2},{4,5},{5,4},{6,7},{7,6},{8,9},{9,8},{10,11... | collective-permute-start | bytes 491528 | tf_op jit(solution)/shard_map/ppermute | solution.py:445
  48.5 8.9 %collective-permute-start.21 = (s32[2,32,640]{2,1,0:T(8,128)S(1)}, s32[2,32,640]{2,1,0:T(8,128)S(1)}, u32[]{:S(2)}, u32[]{:S(2)}) collective-permute-start(s32[2,32,640]{2,1,0:T(8,128)S(1)} %get-tuple-element.138), channel_id=1, source_target_pairs={{0,1},{1,0},{2,3},{3,2},{4,5},{5,4},{6,7},{7,6},{8,9},{9,8},{10,11... | collective-permute-start | bytes 491528 | tf_op jit(solution)/shard_map/ppermute | solution.py:445
  51.0 10.0 %collective-permute-start.1 = (f32[28,1280]{1,0:T(8,128)S(1)}, f32[28,1280]{1,0:T(8,128)S(1)}, u32[]{:S(2)}, u32[]{:S(2)}) collective-permute-start(f32[28,1280]{1,0:T(8,128)S(1)} %get-tuple-element.62), channel_id=1, source_target_pairs={{0,2},{1,3},{2,0},{3,1},{4,6},{5,7},{6,4},{7,5},{8,10},{9,11},{10,... | collective-permute-start | bytes 430088 | tf_op jit(solution)/shard_map/ppermute | solution.py:445
  57.4 14.8 %collective-permute-start.28 = (f32[28,1024]{1,0:T(8,128)S(1)}, f32[28,1024]{1,0:T(8,128)S(1)}, u32[]{:S(2)}, u32[]{:S(2)}) collective-permute-start(f32[28,1024]{1,0:T(8,128)S(1)} %get-tuple-element.85), channel_id=1, source_target_pairs={{0,2},{1,3},{2,0},{3,1},{4,6},{5,7},{6,4},{7,5},{8,10},{9,11},{10,... | collective-permute-start | bytes 344072 | tf_op jit(solution)/shard_map/ppermute | solution.py:445
  61.1 13.6 %collective-permute-start.29 = (f32[28,1024]{1,0:T(8,128)S(1)}, f32[28,1024]{1,0:T(8,128)S(1)}, u32[]{:S(2)}, u32[]{:S(2)}) collective-permute-start(f32[28,1024]{1,0:T(8,128)S(1)} %get-tuple-element.86), channel_id=1, source_target_pairs={{0,8},{1,9},{2,4},{3,5},{4,2},{5,3},{6,14},{7,15},{8,0},{9,1},{10,... | collective-permute-start | bytes 344072 | tf_op jit(solution)/shard_map/ppermute | solution.py:445
  61.2 13.7 %collective-permute-start.24 = (s32[2,24,640]{2,1,0:T(8,128)S(1)}, s32[2,24,640]{2,1,0:T(8,128)S(1)}, u32[]{:S(2)}, u32[]{:S(2)}) collective-permute-start(s32[2,24,640]{2,1,0:T(8,128)S(1)} %get-tuple-element.154), channel_id=1, source_target_pairs={{0,2},{1,3},{2,0},{3,1},{4,6},{5,7},{6,4},{7,5},{8,10},{9,11},{10,... | collective-permute-start | bytes 368648 | tf_op jit(solution)/shard_map/ppermute | solution.py:445
  62.1 13.1 %collective-permute-start.26 = (s32[2,24,640]{2,1,0:T(8,128)S(1)}, s32[2,24,640]{2,1,0:T(8,128)S(1)}, u32[]{:S(2)}, u32[]{:S(2)}) collective-permute-start(s32[2,24,640]{2,1,0:T(8,128)S(1)} %get-tuple-element.152), channel_id=1, source_target_pairs={{0,8},{1,9},{2,4},{3,5},{4,2},{5,3},{6,14},{7,15},{8,0},{9,1},{10,... | collective-permute-start | bytes 368648 | tf_op jit(solution)/shard_map/ppermute | solution.py:445
  62.1 18.5 %collective-permute-start.23 = (s32[2,64,640]{2,1,0:T(8,128)S(1)}, s32[2,64,640]{2,1,0:T(8,128)S(1)}, u32[]{:S(2)}, u32[]{:S(2)}) collective-permute-start(s32[2,64,640]{2,1,0:T(8,128)S(1)} %get-tuple-element.134.whole_m), channel_id=1, source_target_pairs={{0,8},{1,9},{2,10},{3,11},{4,12},{5,13},{6,14},{7,15},{8,0},{9,1},... | collective-permute-start | bytes 983048 | tf_op jit(solution)/shard_map/ppermute | solution.py:445
  79.9 29.2 %collective-permute-start.37 = (s32[2,64,640]{2,1,0:T(8,128)S(1)}, s32[2,64,640]{2,1,0:T(8,128)S(1)}, u32[]{:S(2)}, u32[]{:S(2)}) collective-permute-start(s32[2,64,640]{2,1,0:T(8,128)S(1)} %get-tuple-element.135.whole_m), channel_id=1, source_target_pairs={{0,8},{1,9},{2,10},{3,11},{4,12},{5,13},{6,14},{7,15},{8,0},{9,1},... | collective-permute-start | bytes 983048 | tf_op jit(solution)/shard_map/ppermute | solution.py:445
  80.5 13.8 %collective-permute-start.39 = (s32[2,24,640]{2,1,0:T(8,128)S(1)}, s32[2,24,640]{2,1,0:T(8,128)S(1)}, u32[]{:S(2)}, u32[]{:S(2)}) collective-permute-start(s32[2,24,640]{2,1,0:T(8,128)S(1)} %collective-permute-done.38.a_m), channel_id=1, source_target_pairs={{0,8},{1,9},{2,10},{3,11},{4,12},{5,13},{6,14},{7,15},{8,0},{9,1},... | collective-permute-start | bytes 368648 | tf_op jit(solution)/shard_map/ppermute | solution.py:445
  80.6 15.5 %collective-permute-start.41 = (s32[2,24,640]{2,1,0:T(8,128)S(1)}, s32[2,24,640]{2,1,0:T(8,128)S(1)}, u32[]{:S(2)}, u32[]{:S(2)}) collective-permute-start(s32[2,24,640]{2,1,0:T(8,128)S(1)} %collective-permute-done.40.b_m), channel_id=1, source_target_pairs={{0,8},{1,9},{2,10},{3,11},{4,12},{5,13},{6,14},{7,15},{8,0},{9,1},... | collective-permute-start | bytes 368648 | tf_op jit(solution)/shard_map/ppermute | solution.py:445
  83.1 13.1 %collective-permute-start.18 = (f32[120,128]{1,0:T(8,128)S(1)}, f32[120,128]{1,0:T(8,128)S(1)}, u32[]{:S(2)}, u32[]{:S(2)}) collective-permute-start(f32[120,128]{1,0:T(8,128)S(1)} %get-tuple-element.77), channel_id=1, source_target_pairs={{0,1},{1,0},{2,3},{3,2},{4,5},{5,4},{6,7},{7,6},{8,9},{9,8},{10,11... | collective-permute-start | bytes 184328 | tf_op jit(solution)/shard_map/ppermute | solution.py:445
  84.5 12.4 %collective-permute-start.19 = (f32[120,128]{1,0:T(8,128)S(1)}, f32[120,128]{1,0:T(8,128)S(1)}, u32[]{:S(2)}, u32[]{:S(2)}) collective-permute-start(f32[120,128]{1,0:T(8,128)S(1)} %get-tuple-element.78), channel_id=1, source_target_pairs={{0,8},{1,17},{2,10},{3,19},{4,12},{5,21},{6,14},{7,23},{8,0},{9,25... | collective-permute-start | bytes 184328 | tf_op jit(solution)/shard_map/ppermute | solution.py:445
  94.3 16.9 %collective-permute-start.52 = (s32[2,24,640]{2,1,0:T(8,128)S(1)}, s32[2,24,640]{2,1,0:T(8,128)S(1)}, u32[]{:S(2)}, u32[]{:S(2)}) collective-permute-start(s32[2,24,640]{2,1,0:T(8,128)S(1)} %get-tuple-element.153), channel_id=1, source_target_pairs={{0,2},{1,3},{2,0},{3,1},{4,6},{5,7},{6,4},{7,5},{8,10},{9,11},{10,... | collective-permute-start | bytes 368648 | tf_op jit(solution)/shard_map/ppermute | solution.py:445
  96.1 16.7 %collective-permute-start.54 = (s32[2,24,640]{2,1,0:T(8,128)S(1)}, s32[2,24,640]{2,1,0:T(8,128)S(1)}, u32[]{:S(2)}, u32[]{:S(2)}) collective-permute-start(s32[2,24,640]{2,1,0:T(8,128)S(1)} %get-tuple-element.151), channel_id=1, source_target_pairs={{0,8},{1,9},{2,4},{3,5},{4,2},{5,3},{6,14},{7,15},{8,0},{9,1},{10,... | collective-permute-start | bytes 368648 | tf_op jit(solution)/shard_map/ppermute | solution.py:445
  96.2 10.3 %collective-permute-start.42 = (f32[28,1024]{1,0:T(8,128)S(1)}, f32[28,1024]{1,0:T(8,128)S(1)}, u32[]{:S(2)}, u32[]{:S(2)}) collective-permute-start(f32[28,1024]{1,0:T(8,128)S(1)} %get-tuple-element.97), channel_id=1, source_target_pairs={{0,2},{1,3},{2,0},{3,1},{4,6},{5,7},{6,4},{7,5},{8,10},{9,11},{10,... | collective-permute-start | bytes 344072 | tf_op jit(solution)/shard_map/ppermute | solution.py:445
  96.9 11.5 %collective-permute-start.43 = (f32[28,1024]{1,0:T(8,128)S(1)}, f32[28,1024]{1,0:T(8,128)S(1)}, u32[]{:S(2)}, u32[]{:S(2)}) collective-permute-start(f32[28,1024]{1,0:T(8,128)S(1)} %get-tuple-element.98), channel_id=1, source_target_pairs={{0,8},{1,9},{2,4},{3,5},{4,2},{5,3},{6,14},{7,15},{8,0},{9,1},{10,... | collective-permute-start | bytes 344072 | tf_op jit(solution)/shard_map/ppermute | solution.py:445
  112.8 28.5 %collective-permute-start.51 = (s32[2,64,640]{2,1,0:T(8,128)S(1)}, s32[2,64,640]{2,1,0:T(8,128)S(1)}, u32[]{:S(2)}, u32[]{:S(2)}) collective-permute-start(s32[2,64,640]{2,1,0:T(8,128)S(1)} %get-tuple-element.133.whole_m), channel_id=1, source_target_pairs={{0,8},{1,9},{2,10},{3,11},{4,12},{5,13},{6,14},{7,15},{8,0},{9,1},... | collective-permute-start | bytes 983048 | tf_op jit(solution)/shard_map/ppermute | solution.py:445
  113.1 26.3 %collective-permute-start.53 = (s32[2,24,640]{2,1,0:T(8,128)S(1)}, s32[2,24,640]{2,1,0:T(8,128)S(1)}, u32[]{:S(2)}, u32[]{:S(2)}) collective-permute-start(s32[2,24,640]{2,1,0:T(8,128)S(1)} %collective-permute-done.52.a_m), channel_id=1, source_target_pairs={{0,8},{1,9},{2,10},{3,11},{4,12},{5,13},{6,14},{7,15},{8,0},{9,1},... | collective-permute-start | bytes 368648 | tf_op jit(solution)/shard_map/ppermute | solution.py:445
  113.4 27.7 %collective-permute-start.55 = (s32[2,24,640]{2,1,0:T(8,128)S(1)}, s32[2,24,640]{2,1,0:T(8,128)S(1)}, u32[]{:S(2)}, u32[]{:S(2)}) collective-permute-start(s32[2,24,640]{2,1,0:T(8,128)S(1)} %collective-permute-done.54.b_m), channel_id=1, source_target_pairs={{0,8},{1,9},{2,10},{3,11},{4,12},{5,13},{6,14},{7,15},{8,0},{9,1},... | collective-permute-start | bytes 368648 | tf_op jit(solution)/shard_map/ppermute | solution.py:445
  114.4 11.5 %collective-permute-start.35 = (f32[120,128]{1,0:T(8,128)S(1)}, f32[120,128]{1,0:T(8,128)S(1)}, u32[]{:S(2)}, u32[]{:S(2)}) collective-permute-start(f32[120,128]{1,0:T(8,128)S(1)} %get-tuple-element.94), channel_id=1, source_target_pairs={{0,1},{1,0},{2,3},{3,2},{4,5},{5,4},{6,7},{7,6},{8,9},{9,8},{10,11... | collective-permute-start | bytes 184328 | tf_op jit(solution)/shard_map/ppermute | solution.py:445
  115.9 11.3 %collective-permute-start.36 = (f32[120,128]{1,0:T(8,128)S(1)}, f32[120,128]{1,0:T(8,128)S(1)}, u32[]{:S(2)}, u32[]{:S(2)}) collective-permute-start(f32[120,128]{1,0:T(8,128)S(1)} %get-tuple-element.95), channel_id=1, source_target_pairs={{0,8},{1,17},{2,10},{3,19},{4,12},{5,21},{6,14},{7,23},{8,0},{9,25... | collective-permute-start | bytes 184328 | tf_op jit(solution)/shard_map/ppermute | solution.py:445
  125.9 10.9 %collective-permute-start.56 = (f32[28,1024]{1,0:T(8,128)S(1)}, f32[28,1024]{1,0:T(8,128)S(1)}, u32[]{:S(2)}, u32[]{:S(2)}) collective-permute-start(f32[28,1024]{1,0:T(8,128)S(1)} %get-tuple-element.109), channel_id=1, source_target_pairs={{0,2},{1,3},{2,0},{3,1},{4,6},{5,7},{6,4},{7,5},{8,10},{9,11},{10,... | collective-permute-start | bytes 344072 | tf_op jit(solution)/shard_map/ppermute | solution.py:445
  127.2 11.5 %collective-permute-start.57 = (f32[28,1024]{1,0:T(8,128)S(1)}, f32[28,1024]{1,0:T(8,128)S(1)}, u32[]{:S(2)}, u32[]{:S(2)}) collective-permute-start(f32[28,1024]{1,0:T(8,128)S(1)} %get-tuple-element.110), channel_id=1, source_target_pairs={{0,8},{1,9},{2,4},{3,5},{4,2},{5,3},{6,14},{7,15},{8,0},{9,1},{10,... | collective-permute-start | bytes 344072 | tf_op jit(solution)/shard_map/ppermute | solution.py:445
  141.3 24.1 %collective-permute-start.15 = (f32[4,64,256]{2,1,0:T(8,128)S(1)}, f32[4,64,256]{2,1,0:T(8,128)S(1)}, u32[]{:S(2)}, u32[]{:S(2)}) collective-permute-start(f32[4,64,256]{2,1,0:T(8,128)S(1)} %get-tuple-element.73), channel_id=1, source_target_pairs={{0,8},{1,9},{2,10},{3,11},{4,12},{5,13},{6,14},{7,15},{8,0},{9,1},... | collective-permute-start | bytes 786440 | tf_op jit(solution)/shard_map/ppermute | solution.py:445
  142.9 22.5 %collective-permute-start.32 = (f32[4,64,256]{2,1,0:T(8,128)S(1)}, f32[4,64,256]{2,1,0:T(8,128)S(1)}, u32[]{:S(2)}, u32[]{:S(2)}) collective-permute-start(f32[4,64,256]{2,1,0:T(8,128)S(1)} %get-tuple-element.90), channel_id=1, source_target_pairs={{0,8},{1,9},{2,10},{3,11},{4,12},{5,13},{6,14},{7,15},{8,0},{9,1},... | collective-permute-start | bytes 786440 | tf_op jit(solution)/shard_map/ppermute | solution.py:445
  143.2 22.2 %collective-permute-start.46 = (f32[4,64,256]{2,1,0:T(8,128)S(1)}, f32[4,64,256]{2,1,0:T(8,128)S(1)}, u32[]{:S(2)}, u32[]{:S(2)}) collective-permute-start(f32[4,64,256]{2,1,0:T(8,128)S(1)} %get-tuple-element.102), channel_id=1, source_target_pairs={{0,8},{1,9},{2,10},{3,11},{4,12},{5,13},{6,14},{7,15},{8,0},{9,1},... | collective-permute-start | bytes 786440 | tf_op jit(solution)/shard_map/ppermute | solution.py:445
  144.2 11.1 %collective-permute-start.49 = (f32[120,128]{1,0:T(8,128)S(1)}, f32[120,128]{1,0:T(8,128)S(1)}, u32[]{:S(2)}, u32[]{:S(2)}) collective-permute-start(f32[120,128]{1,0:T(8,128)S(1)} %get-tuple-element.106), channel_id=1, source_target_pairs={{0,1},{1,0},{2,3},{3,2},{4,5},{5,4},{6,7},{7,6},{8,9},{9,8},{10,11... | collective-permute-start | bytes 184328 | tf_op jit(solution)/shard_map/ppermute | solution.py:445
  145.8 9.5 %collective-permute-start.50 = (f32[120,128]{1,0:T(8,128)S(1)}, f32[120,128]{1,0:T(8,128)S(1)}, u32[]{:S(2)}, u32[]{:S(2)}) collective-permute-start(f32[120,128]{1,0:T(8,128)S(1)} %get-tuple-element.107), channel_id=1, source_target_pairs={{0,8},{1,17},{2,10},{3,19},{4,12},{5,21},{6,14},{7,23},{8,0},{9,25... | collective-permute-start | bytes 184328 | tf_op jit(solution)/shard_map/ppermute | solution.py:445
  166.6 8.3 %collective-permute-start.62 = (f32[4,32,256]{2,1,0:T(8,128)S(1)}, f32[4,32,256]{2,1,0:T(8,128)S(1)}, u32[]{:S(2)}, u32[]{:S(2)}) collective-permute-start(f32[4,32,256]{2,1,0:T(8,128)S(1)} %constant_dynamic-slice_fusion.1), channel_id=1, source_target_pairs={{0,1},{1,0},{2,3},{3,2},{4,5},{5,4},{6,7},{7,6},{8,9},{9,8},{10,11... | collective-permute-start | bytes 393224 | tf_op jit(solution)/shard_map/ppermute | solution.py:445
  (38 other events, 202.6 us)
